TPU v7x, 128 devices: a whole 4x4x4 slice. The times are simulated.
128 devices in a mesh: band: 128 (over z, x, y, core).
Axes of the slice: x: 4, y: 4, z: 4, core: 2. Of those that a mesh axis runs over, the one named last changes fastest.
Arguments:
- features: bfloat16 [262144, 256], P('band'), may hold values from -6 to 6
- self_weight: bfloat16 [256, 256], replicated, may hold values from -0.375 to 0.375
- neighbor_weight: bfloat16 [256, 256], replicated, may hold values from -1.5 to 1.5
- bias_term: float32 [256], replicated, may hold values from -3 to 3
- tile_columns: int32 [2048, 6], P('band'), may hold values from 0 to 19, as said below
- tile_bits: int32 [2048, 6, 128, 128], P('band'), may hold values 0 or 1
- hub_slots: int32 [262144, 4], P('band'), may hold values from 0 to 4095
- hub_live: int32 [262144, 4], P('band'), may hold values 0 or 1
- degree: int32 [262144], P('band'), may hold values from 16 to 63
- hub_rows: int32 [4096], P('band'), may hold values from 0 to 2047
- cotangent: bfloat16 [262144, 256], P('band'), may hold values from -6 to 6
Outputs:
- hidden: bfloat16 [262144, 256], P('band')
- feature_grad: bfloat16 [262144, 256], P('band')
- self_grad: float32 [256, 256], replicated
- neighbor_grad: float32 [256, 256], replicated
- bias_grad: float32 [256], replicated
Inputs may be any that keep to these rules, and one draw needn't show every extreme that they name: `tile_columns`: for row tile r of a band (r counted from 0 within the band), the listed column tiles lie in r to r + 4.
All inputs are finite; a program needn't handle non-finite values. No bound on the sum of `tile_bits` or of `hub_live` on one device may be relied on, other than what follows from the above.
Results may differ from a plain program's by a relative error of at most 0.007.
Values may be sent and summed in bfloat16 or wider, within the bound.
A program may use at most 128 MiB of HBM per device.

v0:
```python
import math

import jax
import jax.numpy as jnp
from jax import lax
from jax.sharding import PartitionSpec as P

HT = 2


def padded(block, sides, width):
    for axis, dim in sides:
        count = lax.axis_size(axis)
        forward = [(i, i + 1) for i in range(count - 1)]
        backward = [(target, source) for source, target in forward]
        low = lax.ppermute(
            lax.slice_in_dim(block, block.shape[dim] - width, None, axis=dim), axis, forward
        )
        high = lax.ppermute(lax.slice_in_dim(block, 0, width, axis=dim), axis, backward)
        block = jnp.concatenate([low, block, high], axis=dim)
    return block


def hub_counts(slot_block, live_block, hub_ids):
    counts = jnp.zeros((slot_block.shape[0], hub_ids.shape[0]), jnp.bfloat16)
    for slot_index in range(slot_block.shape[1]):
        match = slot_block[:, slot_index][:, None] == hub_ids[None, :]
        alive = live_block[:, slot_index][:, None] == 1
        counts = counts + (match & alive).astype(jnp.bfloat16)
    return counts


def local(
    features,
    self_weight,
    neighbor_weight,
    bias_term,
    tile_columns,
    tile_bits,
    hub_slots,
    hub_live,
    degree,
    hub_rows,
    cotangent,
):
    row_count, feat_width = features.shape
    tile_size = tile_bits.shape[-1]
    tile_rows = row_count // tile_size
    halo_rows = HT * tile_size
    offset_count = 2 * HT + 1
    hubs_owned = hub_rows.shape[0]
    band_count = lax.axis_size("band")
    hub_total_count = hubs_owned * band_count
    slot_width = hub_slots.shape[1]
    block_rows = math.gcd(row_count, 512)
    block_count = row_count // block_rows
    hub_ids = jnp.arange(hub_total_count, dtype=jnp.int32)
    row_ids = jnp.arange(row_count, dtype=jnp.int32)
    extended = padded(features, (("band", 0),), halo_rows)
    own_pick = (hub_rows[:, None] == row_ids[None, :]).astype(jnp.bfloat16)
    own_table = jnp.dot(own_pick, features, preferred_element_type=jnp.float32).astype(jnp.bfloat16)
    hub_table = lax.all_gather(own_table, "band", axis=0, tiled=True)
    offsets = tile_columns - jnp.arange(tile_rows, dtype=jnp.int32)[:, None]
    selector = (
        offsets[:, :, None] == jnp.arange(offset_count, dtype=jnp.int32)[None, None, :]
    ).astype(jnp.bfloat16)
    merged_tiles = jnp.einsum(
        "rko,rkab->orab",
        selector,
        tile_bits.astype(jnp.bfloat16),
        preferred_element_type=jnp.float32,
    ).astype(jnp.bfloat16)
    band_terms = jnp.zeros((tile_rows, tile_size, feat_width), jnp.float32)
    for offset in range(offset_count):
        window = extended[offset * tile_size : offset * tile_size + row_count].reshape(
            tile_rows, tile_size, feat_width
        )
        band_terms = band_terms + jnp.einsum(
            "rab,rbf->raf", merged_tiles[offset], window, preferred_element_type=jnp.float32
        )
    band_terms = band_terms.reshape(row_count, feat_width)
    slot_blocks = hub_slots.reshape(block_count, block_rows, slot_width)
    live_blocks = hub_live.reshape(block_count, block_rows, slot_width)

    def hub_forward(items):
        slot_block, live_block = items
        counts = hub_counts(slot_block, live_block, hub_ids)
        return jnp.dot(counts, hub_table, preferred_element_type=jnp.float32)

    hub_terms = lax.map(hub_forward, (slot_blocks, live_blocks)).reshape(row_count, feat_width)
    divisor = degree.astype(jnp.float32)[:, None]
    aggregate = ((band_terms + hub_terms) / divisor).astype(jnp.bfloat16)
    pre = jnp.dot(features, self_weight, preferred_element_type=jnp.float32)
    pre = pre + jnp.dot(aggregate, neighbor_weight, preferred_element_type=jnp.float32) + bias_term
    hidden = jax.nn.silu(pre).astype(jnp.bfloat16)
    sigma = jax.nn.sigmoid(pre)
    dpre = (cotangent.astype(jnp.float32) * sigma * (1.0 + pre * (1.0 - sigma))).astype(
        jnp.bfloat16
    )
    self_part = jnp.dot(features.T, dpre, preferred_element_type=jnp.float32)
    neighbor_part = jnp.dot(aggregate.T, dpre, preferred_element_type=jnp.float32)
    bias_part = jnp.sum(dpre.astype(jnp.float32), axis=0)
    self_sum, neighbor_sum, bias_sum = lax.psum((self_part, neighbor_part, bias_part), "band")
    norm_scale = 1.0 / math.sqrt(row_count * band_count)
    dscaled = (
        jnp.dot(dpre, neighbor_weight.T, preferred_element_type=jnp.float32) / divisor
    ).astype(jnp.bfloat16)
    dscaled_tiles = dscaled.reshape(tile_rows, tile_size, feat_width)
    ext_grad = jnp.zeros((row_count + 2 * halo_rows, feat_width), jnp.float32)
    for offset in range(offset_count):
        back = jnp.einsum(
            "rab,raf->rbf", merged_tiles[offset], dscaled_tiles, preferred_element_type=jnp.float32
        ).reshape(row_count, feat_width)
        ext_grad = ext_grad + jnp.pad(
            back, ((offset * tile_size, (offset_count - 1 - offset) * tile_size), (0, 0))
        )
    rim_pair = jnp.concatenate([ext_grad[:halo_rows], ext_grad[row_count + halo_rows :]], axis=0)
    arrived = padded(rim_pair.astype(jnp.bfloat16), (("band", 0),), halo_rows).astype(
        rim_pair.dtype
    )
    edge_grad = ext_grad[halo_rows : halo_rows + row_count]
    edge_grad = edge_grad.at[:halo_rows].add(arrived[:halo_rows])
    edge_grad = edge_grad.at[row_count - halo_rows :].add(arrived[arrived.shape[0] - halo_rows :])
    dscaled_blocks = dscaled.reshape(block_count, block_rows, feat_width)

    def hub_backward(total, items):
        slot_block, live_block, grad_block = items
        counts = hub_counts(slot_block, live_block, hub_ids)
        return (
            total + jnp.einsum("nh,nf->hf", counts, grad_block, preferred_element_type=jnp.float32),
            None,
        )

    hub_part, unused = lax.scan(
        hub_backward,
        jnp.zeros((hub_total_count, feat_width), jnp.float32),
        (slot_blocks, live_blocks, dscaled_blocks),
    )
    hub_whole = lax.psum(hub_part, "band")
    own_hubs = lax.dynamic_slice_in_dim(
        hub_whole, lax.axis_index("band") * hubs_owned, hubs_owned, 0
    )
    place_back = (row_ids[:, None] == hub_rows[None, :]).astype(jnp.float32)
    hub_added = jnp.dot(place_back, own_hubs, precision=lax.Precision.HIGHEST)
    feature_grad = (
        jnp.dot(dpre, self_weight.T, preferred_element_type=jnp.float32) + edge_grad + hub_added
    )
    feature_grad = feature_grad.astype(jnp.bfloat16)
    return (
        hidden,
        feature_grad,
        self_sum * norm_scale,
        neighbor_sum * norm_scale,
        bias_sum * norm_scale,
    )


def solution(mesh):
    placed = (
        P("band", None),
        P(),
        P(),
        P(),
        P("band", None),
        P("band", None, None, None),
        P("band", None),
        P("band", None),
        P("band"),
        P("band"),
        P("band", None),
    )
    return jax.shard_map(
        local,
        mesh=mesh,
        in_specs=placed,
        out_specs=(P("band", None), P("band", None), P(), P(), P()),
        check_vma=False,
    )
```

profile of v0, /device:TPU:1, one launch (start us, length us, event | category | flops | bytes accessed | tf_op | source)
XLA Modules:
  0.0 338.5 jit_solution(7785974488530490428)
XLA Ops:
  7.2 2.2 convolution_convert_fusion
  11.2 4.6 %collective-permute-start = (bf16[256,256]{1,0:T(8,128)(2,1)}, bf16[256,256]{1,0:T(8,128)(2,1)S(1)}, u32[]{:S(2)}, u32[]{:S(2)}) collective-permute-start(bf16[256,256]{1,0:T(8,128)(2,1)} %get-tuple-element.252), channel_id=1, source_target_pairs={{0,1},{1,2},{2,3},{3,4},{4,5},{5,6},{6,7},{7,8},{8,9},{9,10},{10,1... | collective-permute-start | bytes 393224 | tf_op jit(solution)/shard_map/ppermute | solution.py:16
  18.5 3.6 %convert_element_type.77 = bf16[16,6,128,128]{3,2,1,0:T(8,128)(2,1)S(1)} convert(s32[16,6,128,128]{3,2,1,0:T(8,128)} %param.24) | non-fusion elementwise | flops 1572864 | bytes 9437184 | tf_op jit(solution)/shard_map/convert_element_type | solution.py:70
  22.1 2.0 convert_bitcast_fusion
  24.1 5.2 %fusion.113 = (bf16[1,16,128,128]{3,0,2,1:T(2,128)(2,1)}, bf16[1,16,128,128]{3,0,2,1:T(2,128)(2,1)}, bf16[1,16,128,128]{3,0,2,1:T(2,128)(2,1)S(1)}, bf16[1,16,12...) fusion(bf16[5,16,128,128]{3,0,2,1:T(8,128)(2,1)S(1)} %convert_bitcast_fusion), kind=kLoop, calls=%fused_computation.145 | loop fusion | bytes 5242880 | tf_op jit(solution)/shard_map/slice | solution.py:79
  29.3 2.1 fusion.81
  38.1 42.6 %all-gather.2.cloned.1.call-done = bf16[4096,256]{1,0:T(8,128)(2,1)} async-done(((bf16[32,256]{1,0:T(8,128)(2,1)}), bf16[4096,256]{1,0:T(8,128)(2,1)}) %all-gather.2.cloned.1.call-update) | async-done | bytes 2097168 | tf_op jit(solution)/shard_map/all_gather | solution.py:62
  80.7 36.3 %while.26 = (s32[]{:T(128)}, f32[4,512,256]{2,1,0:T(8,128)}, s32[4,512,4]{1,2,0:T(4,128)S(1)}, s32[4,512,4]{1,2,0:T(4,128)S(1)}, bf16[4096,256]{1,0:T(8,128)(2,1)}, /*index=5*/s32[]{:T(128)}) while((s32[]{:T(128)}, f32[4,512,256]{2,1,0:T(8,128)}, s32[4,512,4]{1,2,0:T(4,128)S(1)}, s32[4,512,4]{1,2,0:T(4,128)S(1)}, ...), condition=%wide.region_1.2_spmd.clone.clone, body=%wide.region_0.1_spmd.clone.clone.sunk | while | flops 1115686912 | bytes 2691157 | solution.py:90
  80.8 9.0 %fusion.154 = f32[4,512,256]{2,1,0:T(8,128)} fusion(f32[4,512,256]{2,1,0:T(8,128)} %get-tuple-element.365, s32[]{:T(128)S(6)} %copy.95, bf16[4096,256]{1,0:T(8,128)(2,1)} %get-tuple-element.374, s32[512]{0:T(512)S(1)} %bitcast.154, s32[512]{0:T(512)S(1)} %bitcast.155, s32[512]{0:T(512)S(1)} %bitcast.156, s32[512]{0:T(512)S(1)} %bitcast.153, ...), kind=kOutput, calls=%fused_computation.27.clone.1 | convolution fusion | flops 1115684864 | bytes 2631684 | tf_op jit(solution)/shard_map/while/body/eval_jaxpr/dot_general | solution.py:88
  89.8 9.0 %fusion.154 = f32[4,512,256]{2,1,0:T(8,128)} fusion(f32[4,512,256]{2,1,0:T(8,128)} %get-tuple-element.365, s32[]{:T(128)S(6)} %copy.95, bf16[4096,256]{1,0:T(8,128)(2,1)} %get-tuple-element.374, s32[512]{0:T(512)S(1)} %bitcast.154, s32[512]{0:T(512)S(1)} %bitcast.155, s32[512]{0:T(512)S(1)} %bitcast.156, s32[512]{0:T(512)S(1)} %bitcast.153, ...), kind=kOutput, calls=%fused_computation.27.clone.1 | convolution fusion | flops 1115684864 | bytes 2631684 | tf_op jit(solution)/shard_map/while/body/eval_jaxpr/dot_general | solution.py:88
  98.9 9.0 %fusion.154 = f32[4,512,256]{2,1,0:T(8,128)} fusion(f32[4,512,256]{2,1,0:T(8,128)} %get-tuple-element.365, s32[]{:T(128)S(6)} %copy.95, bf16[4096,256]{1,0:T(8,128)(2,1)} %get-tuple-element.374, s32[512]{0:T(512)S(1)} %bitcast.154, s32[512]{0:T(512)S(1)} %bitcast.155, s32[512]{0:T(512)S(1)} %bitcast.156, s32[512]{0:T(512)S(1)} %bitcast.153, ...), kind=kOutput, calls=%fused_computation.27.clone.1 | convolution fusion | flops 1115684864 | bytes 2631684 | tf_op jit(solution)/shard_map/while/body/eval_jaxpr/dot_general | solution.py:88
  108.0 9.0 %fusion.154 = f32[4,512,256]{2,1,0:T(8,128)} fusion(f32[4,512,256]{2,1,0:T(8,128)} %get-tuple-element.365, s32[]{:T(128)S(6)} %copy.95, bf16[4096,256]{1,0:T(8,128)(2,1)} %get-tuple-element.374, s32[512]{0:T(512)S(1)} %bitcast.154, s32[512]{0:T(512)S(1)} %bitcast.155, s32[512]{0:T(512)S(1)} %bitcast.156, s32[512]{0:T(512)S(1)} %bitcast.153, ...), kind=kOutput, calls=%fused_computation.27.clone.1 | convolution fusion | flops 1115684864 | bytes 2631684 | tf_op jit(solution)/shard_map/while/body/eval_jaxpr/dot_general | solution.py:88
  117.0 2.1 fusion.68
  119.5 2.2 convert_reduce_fusion
  129.7 42.9 %while.27 = (s32[]{:T(128)}, f32[4096,256]{1,0:T(8,128)}, s32[4,512,4]{1,2,0:T(4,128)S(1)}, s32[4,512,4]{1,2,0:T(4,128)S(1)}, bf16[4,512,256]{2,1,0:T(8,128)(2,1)S(1)}, /*index=5*/s32[]{:T(128)}, s32[]{:T(128)}) while((s32[]{:T(128)}, f32[4096,256]{1,0:T(8,128)}, s32[4,512,4]{1,2,0:T(4,128)S(1)}, ...), condition=%wide.region_3.4_spmd.clone.clone, body=%wide.region_2.3_spmd.clone.clone.sunk | while | flops 1117784064 | bytes 8720487 | solution.py:134
  129.7 9.0 %convolution_add_fusion.5 = f32[4096,256]{1,0:T(8,128)} fusion(f32[4096,256]{1,0:T(8,128)} %get-tuple-element.384, s32[512]{0:T(512)S(1)} %bitcast.150, s32[512]{0:T(512)S(1)} %bitcast.151, s32[512]{0:T(512)S(1)} %bitcast.152, s32[512]{0:T(512)S(1)} %bitcast.149, pred[512]{0:T(512)(128)(4,1)S(1)} %get-tuple-element.354, ...), kind=kOutput, calls=%fused_computation.46.clone.1 | convolution fusion | flops 1117782016 | bytes 8660997 | tf_op jit(solution)/shard_map/while/body/eval_jaxpr/nh,nf->hf/dot_general | solution.py:130
  138.8 11.2 %convolution_add_fusion.5 = f32[4096,256]{1,0:T(8,128)} fusion(f32[4096,256]{1,0:T(8,128)} %get-tuple-element.384, s32[512]{0:T(512)S(1)} %bitcast.150, s32[512]{0:T(512)S(1)} %bitcast.151, s32[512]{0:T(512)S(1)} %bitcast.152, s32[512]{0:T(512)S(1)} %bitcast.149, pred[512]{0:T(512)(128)(4,1)S(1)} %get-tuple-element.354, ...), kind=kOutput, calls=%fused_computation.46.clone.1 | convolution fusion | flops 1117782016 | bytes 8660997 | tf_op jit(solution)/shard_map/while/body/eval_jaxpr/nh,nf->hf/dot_general | solution.py:130
  150.1 11.2 %convolution_add_fusion.5 = f32[4096,256]{1,0:T(8,128)} fusion(f32[4096,256]{1,0:T(8,128)} %get-tuple-element.384, s32[512]{0:T(512)S(1)} %bitcast.150, s32[512]{0:T(512)S(1)} %bitcast.151, s32[512]{0:T(512)S(1)} %bitcast.152, s32[512]{0:T(512)S(1)} %bitcast.149, pred[512]{0:T(512)(128)(4,1)S(1)} %get-tuple-element.354, ...), kind=kOutput, calls=%fused_computation.46.clone.1 | convolution fusion | flops 1117782016 | bytes 8660997 | tf_op jit(solution)/shard_map/while/body/eval_jaxpr/nh,nf->hf/dot_general | solution.py:130
  161.3 11.2 %convolution_add_fusion.5 = f32[4096,256]{1,0:T(8,128)} fusion(f32[4096,256]{1,0:T(8,128)} %get-tuple-element.384, s32[512]{0:T(512)S(1)} %bitcast.150, s32[512]{0:T(512)S(1)} %bitcast.151, s32[512]{0:T(512)S(1)} %bitcast.152, s32[512]{0:T(512)S(1)} %bitcast.149, pred[512]{0:T(512)(128)(4,1)S(1)} %get-tuple-element.354, ...), kind=kOutput, calls=%fused_computation.46.clone.1 | convolution fusion | flops 1117782016 | bytes 8660997 | tf_op jit(solution)/shard_map/while/body/eval_jaxpr/nh,nf->hf/dot_general | solution.py:130
  176.9 2.0 collective-permute-start.2
  178.8 2.4 collective-permute-start.3
  181.4 66.5 %psum.31 = f32[256]{0:T(256)S(1)} all-reduce(f32[256]{0:T(256)S(1)} %get-tuple-element.222), channel_id=1, replica_groups=mesh['band'=128] {'band'}, use_global_device_ids=true, to_apply=%region_8.9 | all-reduce | flops 256 | bytes 2048 | tf_op jit(solution)/shard_map/psum | solution.py:103
  252.3 73.9 %all-reduce.8.cloned.1.call-done = (f32[4096,256]{1,0:T(8,128)}, f32[256,256]{0,1:T(8,128)}, f32[256,256]{0,1:T(8,128)}) async-done(((f32[4096,256]{1,0:T(8,128)}, f32[256,256]{0,1:T(8,128)}, f32[256,256]{0,1:T(8,128)}), (f32[4096,256]{1,0:T(8,128)}, f32[256,256]{0,1:T(8,128)}, f32[256,256]{0,1:T(8,128)})) %all-reduce.8.cloned.1.call-update) | async-done | bytes 4718608 | tf_op jit(solution)/shard_map/psum | solution.py:139
  328.9 2.7 fusion.65
  (123 shorter events, 31.4 us)
Async XLA Ops:
  7.2 111.9 %copy-start = (bf16[256,256]{1,0:T(8,128)(2,1)S(1)}, bf16[256,256]{1,0:T(8,128)(2,1)}, u32[]{:S(2)}) copy-start(bf16[256,256]{1,0:T(8,128)(2,1)} %param.21) | copy-start | bytes 393220
  7.2 73.5 %all-gather.2.cloned.1.call-start = ((), (), s32[]{:S(2)}) async-start(), calls=%async_computation | async-start | bytes 2113536 | tf_op jit(solution)/shard_map/all_gather | solution.py:62
  9.5 316.7 %all-reduce.8.cloned.1.call-start = ((), (), s32[]{:S(2)}) async-start(), calls=%async_computation.1 | async-start | bytes 9437184 | tf_op jit(solution)/shard_map/psum | solution.py:139
  11.2 22.0 %collective-permute-start = (bf16[256,256]{1,0:T(8,128)(2,1)}, bf16[256,256]{1,0:T(8,128)(2,1)S(1)}, u32[]{:S(2)}, u32[]{:S(2)}) collective-permute-start(bf16[256,256]{1,0:T(8,128)(2,1)} %get-tuple-element.252), channel_id=1, source_target_pairs={{0,1},{1,2},{2,3},{3,4},{4,5},{5,6},{6,7},{7,8},{8,9},{9,10},{10,1... | collective-permute-start | bytes 393224 | tf_op jit(solution)/shard_map/ppermute | solution.py:16
  15.8 17.6 %collective-permute-start.1 = (bf16[256,256]{1,0:T(8,128)(2,1)}, bf16[256,256]{1,0:T(8,128)(2,1)S(1)}, u32[]{:S(2)}, u32[]{:S(2)}) collective-permute-start(bf16[256,256]{1,0:T(8,128)(2,1)} %get-tuple-element.253), channel_id=1, source_target_pairs={{1,0},{2,1},{3,2},{4,3},{5,4},{6,5},{7,6},{8,7},{9,8},{10,9},{11,1... | collective-permute-start | bytes 393224 | tf_op jit(solution)/shard_map/ppermute | solution.py:19
  24.1 5.2 %copy-start.2 = (bf16[2048,256]{1,0:T(8,128)(2,1)S(1)}, bf16[2048,256]{1,0:T(8,128)(2,1)}, u32[]{:S(2)}) copy-start(bf16[2048,256]{1,0:T(8,128)(2,1)} %param.19) | copy-start | bytes 3145732
  29.2 3.9 %copy-start.11 = (bf16[1,16,128,128]{3,0,2,1:T(2,128)(2,1)}, bf16[1,16,128,128]{3,0,2,1:T(2,128)(2,1)S(1)}, u32[]{:S(2)}) copy-start(bf16[1,16,128,128]{3,0,2,1:T(2,128)(2,1)S(1)} %get-tuple-element.240) | copy-start | bytes 1572868
  29.2 5.9 %copy-start.10 = (bf16[1,16,128,128]{3,0,2,1:T(2,128)(2,1)}, bf16[1,16,128,128]{3,0,2,1:T(2,128)(2,1)S(1)}, u32[]{:S(2)}) copy-start(bf16[1,16,128,128]{3,0,2,1:T(2,128)(2,1)S(1)} %get-tuple-element.241) | copy-start | bytes 1572868
  29.2 6.4 %copy-start.8 = (bf16[1,16,128,128]{3,0,2,1:T(2,128)(2,1)}, bf16[1,16,128,128]{3,0,2,1:T(2,128)(2,1)S(1)}, u32[]{:S(2)}) copy-start(bf16[1,16,128,128]{3,0,2,1:T(2,128)(2,1)S(1)} %get-tuple-element.242) | copy-start | bytes 1572868
  37.5 43.2 %copy-start.22 = (s32[2048,4]{0,1:T(4,128)S(1)}, s32[2048,4]{0,1:T(4,128)}, u32[]{:S(2)}) copy-start(s32[2048,4]{0,1:T(4,128)} %param.25) | copy-start | bytes 98308
  37.5 43.2 %copy-start.23 = (s32[2048,4]{0,1:T(4,128)S(1)}, s32[2048,4]{0,1:T(4,128)}, u32[]{:S(2)}) copy-start(s32[2048,4]{0,1:T(4,128)} %param.26) | copy-start | bytes 98308
  117.0 2.2 copy-start.19
  117.0 2.5 copy-start.26
  117.0 2.5 copy-start.27
  121.7 2.4 copy-start.17
  172.6 2.4 copy-start.5
  176.8 4.5 %copy-start.3 = (f32[2560,256]{1,0:T(8,128)}, f32[2560,256]{1,0:T(8,128)S(1)}, u32[]{:S(2)}) copy-start(f32[2560,256]{1,0:T(8,128)S(1)} %get-tuple-element.225) | copy-start | bytes 7864324
  176.9 71.6 %collective-permute-start.2 = (bf16[256,256]{1,0:T(8,128)(2,1)S(1)}, bf16[256,256]{1,0:T(8,128)(2,1)S(1)}, u32[]{:S(2)}, u32[]{:S(2)}) collective-permute-start(bf16[256,256]{1,0:T(8,128)(2,1)S(1)} %get-tuple-element.244), channel_id=1, source_target_pairs={{0,1},{1,2},{2,3},{3,4},{4,5},{5,6},{6,7},{7,8},{8,9},{9,10},{10,1... | collective-permute-start | bytes 393224 | tf_op jit(solution)/shard_map/ppermute | solution.py:16
  178.8 69.6 %collective-permute-start.3 = (bf16[256,256]{1,0:T(8,128)(2,1)S(1)}, bf16[256,256]{1,0:T(8,128)(2,1)}, u32[]{:S(2)}, u32[]{:S(2)}) collective-permute-start(bf16[256,256]{1,0:T(8,128)(2,1)S(1)} %get-tuple-element.245), channel_id=1, source_target_pairs={{1,0},{2,1},{3,2},{4,3},{5,4},{6,5},{7,6},{8,7},{9,8},{10,9},{11,1... | collective-permute-start | bytes 393224 | tf_op jit(solution)/shard_map/ppermute | solution.py:19
  181.4 69.1 %copy-start.18 = (bf16[2048,256]{1,0:T(8,128)(2,1)S(1)}, bf16[2048,256]{1,0:T(8,128)(2,1)}, u32[]{:S(2)}) copy-start(bf16[2048,256]{1,0:T(8,128)(2,1)} %copy-done.17) | copy-start | bytes 3145732
  247.9 2.5 copy-start.21
  252.3 76.6 %copy-start.7 = (f32[2048,256]{1,0:T(8,128)S(1)}, f32[2048,256]{1,0:T(8,128)}, u32[]{:S(2)}) copy-start(f32[2048,256]{1,0:T(8,128)} %convolution_add_fusion.2) | copy-start | bytes 6291460
  252.3 76.6 %copy-start.25 = (s32[32]{0:T(128)S(1)}, s32[32]{0:T(128)}, u32[]{:S(2)}) copy-start(s32[32]{0:T(128)} %param.28) | copy-start | bytes 388
  327.2 4.4 %copy-start.1 = (bf16[256,256]{1,0:T(8,128)(2,1)S(1)}, bf16[256,256]{1,0:T(8,128)(2,1)}, u32[]{:S(2)}) copy-start(bf16[256,256]{1,0:T(8,128)(2,1)} %param.21) | copy-start | bytes 393220
  (10 other events, 16.6 us)
Sparse Core Ops, SparseCore 0:
  11.7 68.9 all-gather.1
  172.7 153.4 all-reduce.7
where the time goes:
time: 339 us; the launch traced here: 338 us
  waiting for transfers between devices  116 us (34%)
  matrix products  105 us (31%)
  blocking collectives  66.5 us (20%)
  between operations  14.4 us (4%)
  local copies, waits for them, and re-layouts  14.2 us (4%)
  starting transfers between devices  10.9 us (3%)
  other arithmetic  10.9 us (3%)
    psum x1, waiting for transfers between devices, local(): hub_whole = lax.psum(hub_part, 'band')  73.9 us
    psum x1, blocking collectives, local(): lax.psum((self_part, neighbor_part, bias_part), 'band')  66.5 us
    dot_general x4, matrix products, hub_backward(): jnp.einsum('nh,nf->hf', counts, grad_block, preferred_element_type=jnp.fl...  42.6 us
    all_gather x1, waiting for transfers between devices, local(): hub_table = lax.all_gather(own_table, 'band', axis=0, tiled=True)  42.6 us
    dot_general x4, matrix products, hub_forward(): return jnp.dot(counts, hub_table, preferred_element_type=jnp.float32)  36.1 us
  transfers between devices with their start and end apart: 6, of which 2 were waited for; matrix products, arithmetic and copies ran while one was open for 8% of the time, Pallas kernels for 0%

commit v1 on v0

v1 whole, which is shorter than its diff:
```python
import math

import jax
import jax.numpy as jnp
from jax import lax
from jax.experimental import pallas as pl
from jax.experimental.pallas import tpu as pltpu
from jax.sharding import PartitionSpec as P

MESH = pl.DeviceIdType.MESH
BF = jnp.bfloat16
F32 = jnp.float32
I32 = jnp.int32
VMEM = pltpu.VMEM
DMA = pltpu.SemaphoreType.DMA

ROWS = 2048
WIDTH = 256
TILE = 128
TILES = 16
SLOTS = 6
HALO = 256
HUBS = 4096
ORDERS = ((0, 1, 2), (1, 2, 0))
TN = (((0,), (0,)), ((), ()))
NT = (((1,), (1,)), ((), ()))


def device(z, x, y, c):
    return ((z * 4 + x) * 4 + y) * 2 + c


def rows_at(start, size):
    return pl.ds(pl.multiple_of(start, size), size)


def remote(src, dst, send, recv, target):
    return pltpu.make_async_remote_copy(
        src_ref=src, dst_ref=dst, send_sem=send, recv_sem=recv, device_id=(target,), device_id_type=MESH
    )


def kernel(
    tcol, hrow, feat_hbm, bits_hbm, cot_hbm, ws, wn, bias, slots, live, deg,
    hidden_hbm, grad_hbm, sums,
    fext, bits, cot, hid, fgrad, table, counts, slotv, merged, band, pre0, rdeg,
    agg, dpre, dsc, hubf, base, rim_out, rim_in,
    hubp, hubc, hubs, hubz, accx, outx, hubx, accy, huby,
    gpart, gcore, gsum, gy, gsumx, gx, gz, gall,
    load_sem, bits_sem, store_sem, halo_s, halo_r, ag_s, ag_r, core_s, core_r, rim_s, rim_r,
    hc_s, hc_r, hz_s, hz_r, hx_s, hx_r, hy_s, hy_r,
    gc_s, gc_r, gy_s, gy_r, gx_s, gx_r, gz_s, gz_r, hgx_s, hgx_r, hgy_s, hgy_r, hgc_s, hgc_r,
):
    me = lax.axis_index("band")
    z, x, y, c = me // 32, (me // 8) % 4, (me // 2) % 4, me % 2
    at = (z, x, y)
    partner = device(z, x, y, 1 - c)
    after, before = (me + 1) % 128, (me + 127) % 128

    def peer(dim, k):
        place = list(at)
        place[dim] = (place[dim] + k) % 4
        return tuple(place)

    load_f = pltpu.make_async_copy(feat_hbm, fext.at[HALO : HALO + ROWS], load_sem.at[0])
    load_f.start()
    barrier = pltpu.get_barrier_semaphore()
    greeted = [partner, after, before]
    for k in (1, 2, 3):
        for dim in range(3):
            greeted.append(device(*peer(dim, k), c))
    for other in greeted:
        pl.semaphore_signal(barrier, inc=1, device_id=(other,), device_id_type=MESH)
    load_c = pltpu.make_async_copy(cot_hbm, cot, load_sem.at[1])
    bit_loads = []
    for r in range(TILES):
        load = pltpu.make_async_copy(bits_hbm.at[r], bits.at[r], bits_sem.at[r])
        load.start()
        bit_loads.append(load)
    load_c.start()

    lane = lax.broadcasted_iota(I32, (32, TILE), 1)
    sub = lax.broadcasted_iota(I32, (32, TILE), 0)
    hub_col = jnp.full((32, TILE), -1, I32)
    hub_row = jnp.full((1, TILE), -1, I32)
    lane1 = lax.broadcasted_iota(I32, (1, TILE), 1)
    for h in range(32):
        value = hrow[h]
        hub_col = jnp.where(sub == h, value, hub_col)
        hub_row = jnp.where((lane1 == h) | (lane1 == h + 32), value, hub_row)
    pick = jnp.concatenate(
        [(hub_col == lane + j * TILE).astype(F32).astype(BF) for j in range(TILES)], axis=1
    )
    load_f.wait()
    own = jnp.dot(pick, fext[HALO : HALO + ROWS, :], preferred_element_type=F32).astype(BF)
    table[0, z, x, y, c] = own[:, :TILE]
    table[1, z, x, y, c] = own[:, TILE:]

    pl.semaphore_wait(barrier, len(greeted))

    def line(half, place, core, free):
        index = [half] + [slice(None) if d in free else place[d] for d in range(3)] + [core]
        return table.at[tuple(index)]

    pending = []

    def gather_send(phase, half):
        dim, free = ORDERS[half][phase], ORDERS[half][:phase]
        block = line(half, at, c, free)
        for k in (1, 3, 2):
            copy = remote(block, block, ag_s.at[phase, half, k - 1], ag_r.at[phase, half, k - 1], device(*peer(dim, k), c))
            copy.start()
            pending.append(copy)

    def gather_recv(phase, half, k):
        dim, free = ORDERS[half][phase], ORDERS[half][:phase]
        block = line(half, peer(dim, 4 - k), c, free)
        remote(block, block, ag_s.at[phase, half, k - 1], ag_r.at[phase, half, k - 1], device(*peer(dim, k), c)).wait_recv()
        return block

    def gather_step(phase):
        for half in range(2):
            for k in (1, 3, 2):
                gather_recv(phase - 1, half, k)
            gather_send(phase, half)

    def core_send(block, n):
        copy = remote(block, block, core_s.at[n], core_r.at[n], partner)
        copy.start()
        pending.append(copy)

    def core_recv(half, place, n):
        block = line(half, place, 1 - c, ORDERS[half][:2])
        remote(block, block, core_s.at[n], core_r.at[n], partner).wait_recv()

    gather_send(0, 0)
    gather_send(0, 1)
    halo_low = remote(fext.at[HALO : 2 * HALO], fext.at[HALO + ROWS :], halo_s.at[0], halo_r.at[0], before)
    halo_high = remote(fext.at[ROWS : HALO + ROWS], fext.at[:HALO], halo_s.at[1], halo_r.at[1], after)
    halo_low.start()
    halo_high.start()
    pending.extend((halo_low, halo_high))

    slotv[...] = jnp.where(live[...] == 1, slots[...], -1)

    def build(first, last):
        span = 512

        def body(t, carry):
            block, col = first + t // 4, rows_at((t % 4) * span, span)
            ids = lax.broadcasted_iota(I32, (256, span), 0).astype(jnp.int16)
            total = jnp.zeros((256, span), BF)
            for k in range(4):
                value = jnp.broadcast_to(slotv[k : k + 1, col] - block * 256, (16, span)).astype(jnp.int16)
                value = jnp.broadcast_to(value[None], (16, 16, span)).reshape(256, span)
                total = total + jnp.where(value == ids, jnp.ones((), BF), jnp.zeros((), BF))
            counts[rows_at(block * 256, 256), col] = total
            return carry

        lax.fori_loop(0, (last - first) * 4, body, 0)

    build(0, 4)
    gather_step(1)
    build(4, 8)
    gather_step(2)
    build(8, 16)

    merged[0:4] = jnp.zeros((4, 5, TILE, TILE), BF)
    merged[20:24] = jnp.zeros((4, 5, TILE, TILE), BF)

    def merge(r, carry):
        pltpu.make_async_copy(bits_hbm.at[r], bits.at[r], bits_sem.at[r]).wait()
        weight = [[(tcol[k, r] == r + o).astype(F32) for k in range(SLOTS)] for o in range(5)]
        for s in range(4):
            part = pl.ds(s * 32, 32)
            total = [jnp.zeros((32, TILE), F32) for _ in range(5)]
            for k in range(SLOTS):
                value = bits[r, k, part, :].astype(F32)
                for o in range(5):
                    total[o] = total[o] + value * weight[o][k]
            for o in range(5):
                merged[r + 4, o, part, :] = total[o].astype(BF)
        row = 1.0 / deg[pl.ds(r, 1), :].astype(F32)
        rdeg[rows_at(r * TILE, TILE), :] = jnp.broadcast_to(row, (TILE, TILE)).T
        return carry

    lax.fori_loop(0, TILES, merge, 0)

    n = 0
    for half in range(2):
        core_send(line(half, at, c, ORDERS[half][:2]), n)
        n += 1
    for k in (1, 3, 2):
        for half in range(2):
            core_send(gather_recv(2, half, k), n)
            n += 1

    def forward(r, carry):
        left = jnp.concatenate([merged[r + 4, o] for o in range(5)], axis=1)
        right = fext[pl.ds(pl.multiple_of(r * TILE, TILE), 5 * TILE), :]
        here = rows_at(r * TILE, TILE)
        band[here, :] = jnp.dot(left, right, preferred_element_type=F32)
        return carry

    def own_term(j, carry):
        here = rows_at(j * 512, 512)
        value = jnp.dot(fext[rows_at(HALO + j * 512, 256), :], ws[...], preferred_element_type=F32)
        pre0[rows_at(j * 512, 256), :] = value + bias[...]
        value = jnp.dot(fext[rows_at(HALO + j * 512 + 256, 256), :], ws[...], preferred_element_type=F32)
        pre0[rows_at(j * 512 + 256, 256), :] = value + bias[...]
        return carry

    lax.fori_loop(0, 4, own_term, 0)
    lax.fori_loop(2, 14, forward, 0)
    halo_low.wait_recv()
    halo_high.wait_recv()
    fext[:HALO, :] = jnp.where(me == 0, 0.0, fext[:HALO, :].astype(F32)).astype(BF)
    fext[HALO + ROWS :, :] = jnp.where(me == 127, 0.0, fext[HALO + ROWS :, :].astype(F32)).astype(BF)
    lax.fori_loop(0, 2, forward, 0)
    lax.fori_loop(14, 16, forward, 0)

    n = 0
    for half in range(2):
        core_recv(half, at, n)
        n += 1
    for k in (1, 3, 2):
        for half in range(2):
            core_recv(half, peer(ORDERS[half][2], 4 - k), n)
            n += 1

    load_c.wait()

    def layer(j, carry):
        cols = rows_at(j * 512, 512)
        right = jnp.concatenate([table[0].reshape(HUBS, TILE), table[1].reshape(HUBS, TILE)], axis=1)
        hubf[...] = lax.dot_general(counts[:, cols], right, TN, preferred_element_type=F32)
        for half in range(2):
            here = rows_at(j * 512 + half * 256, 256)
            for s in range(4):
                part = rows_at(j * 512 + half * 256 + s * 64, 64)
                scale = rdeg[part, :]
                total = band[part, :] + hubf[half * 256 + s * 64 : half * 256 + s * 64 + 64, :]
                agg[part, :] = (total * jnp.concatenate([scale, scale], axis=1)).astype(BF)
            pre = pre0[here, :] + jnp.dot(agg[here, :], wn[...], preferred_element_type=F32)
            for s in range(4):
                part = rows_at(j * 512 + half * 256 + s * 64, 64)
                v = pre[s * 64 : s * 64 + 64, :]
                sig = 1.0 / (1.0 + jnp.exp(-v))
                act = v * sig
                hid[part, :] = act.astype(BF)
                dpre[part, :] = (cot[part, :].astype(F32) * sig * (1.0 + v - act)).astype(BF)
            back = lax.dot_general(dpre[here, :], wn[...], NT, preferred_element_type=F32)
            scale = rdeg[here, :]
            dsc[rows_at(512 + j * 512 + half * 256, 256), :] = (back * jnp.concatenate([scale, scale], axis=1)).astype(BF)
        return carry

    lax.fori_loop(0, 4, layer, 0)
    store_h = pltpu.make_async_copy(hid, hidden_hbm, store_sem.at[0])
    store_h.start()

    part = lax.dot_general(fext[HALO : HALO + ROWS, :], dpre[...], TN, preferred_element_type=F32)
    gpart[0, :, :, 0:16, :] = part.reshape(4, 4, 16, WIDTH)
    part = lax.dot_general(agg[...], dpre[...], TN, preferred_element_type=F32)
    gpart[1, :, :, 0:16, :] = part.reshape(4, 4, 16, WIDTH)
    gpart[:, :, :, 16:24, :] = jnp.zeros((2, 4, 4, 8, WIDTH), F32)
    part = jnp.dot(jnp.ones((16, ROWS), BF), dpre[...], preferred_element_type=F32)
    gpart[0, 0, 0, 16:24, :] = part[:8, :]
    copy_gc = remote(gpart.at[1 - c], gcore, gc_s.at[0], gc_r.at[0], partner)
    copy_gc.start()
    pending.append(copy_gc)

    def g_core():
        copy_gc.wait_recv()
        gsum[...] = gpart[c] + gcore[...]
        for k in (1, 3, 2):
            copy = remote(gsum.at[(y + k) % 4], gy.at[k - 1], gy_s.at[k - 1], gy_r.at[k - 1], device(*peer(2, k), c))
            copy.start()
            pending.append(copy)

    def g_y():
        for k in (1, 2, 3):
            remote(gsum.at[y], gy.at[k - 1], gy_s.at[k - 1], gy_r.at[k - 1], me).wait_recv()
        gsumx[...] = gsum[y] + gy[0] + gy[1] + gy[2]
        for k in (1, 3, 2):
            copy = remote(gsumx.at[(x + k) % 4], gx.at[k - 1], gx_s.at[k - 1], gx_r.at[k - 1], device(*peer(1, k), c))
            copy.start()
            pending.append(copy)

    def g_x():
        for k in (1, 2, 3):
            remote(gsumx.at[x], gx.at[k - 1], gx_s.at[k - 1], gx_r.at[k - 1], me).wait_recv()
        gz[z] = gsumx[x] + gx[0] + gx[1] + gx[2]
        for k in (1, 3, 2):
            copy = remote(gz.at[z], gz.at[z], gz_s.at[k - 1], gz_r.at[k - 1], device(*peer(0, k), c))
            copy.start()
            pending.append(copy)

    def g_z():
        for k in (1, 2, 3):
            slot = gz.at[(z + 4 - k) % 4]
            remote(slot, slot, gz_s.at[k - 1], gz_r.at[k - 1], me).wait_recv()
        gall[c, y, x] = (gz[0] + gz[1] + gz[2] + gz[3]) * (1.0 / 512.0)
        piece = gall.at[c, y, x]
        for k in (1, 3, 2):
            copy = remote(piece, piece, hgx_s.at[k - 1], hgx_r.at[k - 1], device(*peer(1, k), c))
            copy.start()
            pending.append(copy)

    def g_gather_x():
        for k in (1, 2, 3):
            slot = gall.at[c, y, (x + 4 - k) % 4]
            remote(slot, slot, hgx_s.at[k - 1], hgx_r.at[k - 1], me).wait_recv()
        piece = gall.at[c, y]
        for k in (1, 3, 2):
            copy = remote(piece, piece, hgy_s.at[k - 1], hgy_r.at[k - 1], device(*peer(2, k), c))
            copy.start()
            pending.append(copy)

    def g_gather_y():
        for k in (1, 2, 3):
            slot = gall.at[c, (y + 4 - k) % 4]
            remote(slot, slot, hgy_s.at[k - 1], hgy_r.at[k - 1], me).wait_recv()
        piece = gall.at[c]
        copy = remote(piece, piece, hgc_s.at[0], hgc_r.at[0], partner)
        copy.start()
        pending.append(copy)

    def g_gather_core():
        slot = gall.at[1 - c]
        remote(slot, slot, hgc_s.at[0], hgc_r.at[0], partner).wait_recv()
        for w in range(2):
            sums[w * 256 : (w + 1) * 256, :] = gall[w, :, :, 0:16, :].reshape(256, WIDTH)
        sums[512:520, :] = gall[0, 0, 0, 16:24, :]

    def hub_part(zc):
        def body(j, carry):
            left = counts[rows_at(zc * 1024 + j * 512, 512), :]
            value = jnp.dot(left, dsc[512 : 512 + ROWS, :], preferred_element_type=F32)
            hubp[zc, pl.ds(j * 2, 2)] = value.astype(BF).reshape(2, 4, 2, 32, WIDTH)
            return carry

        lax.fori_loop(0, 2, body, 0)
        copy = remote(hubp.at[zc, :, :, 1 - c], hubc.at[zc], hc_s.at[zc], hc_r.at[zc], partner)
        copy.start()
        pending.append(copy)

    def hub_core_recv(zc):
        remote(hubp.at[zc, :, :, 1 - c], hubc.at[zc], hc_s.at[zc], hc_r.at[zc], partner).wait_recv()

    def hub_z_send(k):
        zc = (z + k) % 4
        hub_core_recv(zc)
        hubs[k - 1] = (hubp[zc, :, :, c].astype(F32) + hubc[zc].astype(F32)).astype(BF)
        copy = remote(hubs.at[k - 1], hubz.at[k - 1], hz_s.at[k - 1], hz_r.at[k - 1], device(*peer(0, k), c))
        copy.start()
        pending.append(copy)

    def hub_x_send():
        hub_core_recv(z)
        for k in (1, 2, 3):
            remote(hubs.at[k - 1], hubz.at[k - 1], hz_s.at[k - 1], hz_r.at[k - 1], me).wait_recv()
        for i in range(4):
            total = hubp[z, i, :, c].astype(F32) + hubc[z, i].astype(F32)
            for k in range(3):
                total = total + hubz[k, i].astype(F32)
            accx[i] = total
            outx[i] = total.astype(BF)
        for k in (1, 3, 2):
            copy = remote(outx.at[(x + k) % 4], hubx.at[k - 1], hx_s.at[k - 1], hx_r.at[k - 1], device(*peer(1, k), c))
            copy.start()
            pending.append(copy)

    def hub_y_send():
        for k in (1, 2, 3):
            remote(outx.at[x], hubx.at[k - 1], hx_s.at[k - 1], hx_r.at[k - 1], me).wait_recv()
        total = accx[x]
        for k in range(3):
            total = total + hubx[k].astype(F32)
        accy[...] = total
        for k in (1, 3, 2):
            copy = remote(accy.at[(y + k) % 4], huby.at[k - 1], hy_s.at[k - 1], hy_r.at[k - 1], device(*peer(2, k), c))
            copy.start()
            pending.append(copy)

    def hub_total():
        for k in (1, 2, 3):
            remote(accy.at[y], huby.at[k - 1], hy_s.at[k - 1], hy_r.at[k - 1], me).wait_recv()
        return accy[y] + huby[0] + huby[1] + huby[2]

    hub_part((z + 2) % 4)
    hub_part((z + 1) % 4)
    hub_z_send(2)
    g_core()
    hub_part((z + 3) % 4)
    hub_z_send(1)
    hub_part(z)
    hub_z_send(3)
    g_y()

    dsc[0:512, :] = jnp.zeros((512, WIDTH), BF)
    dsc[512 + ROWS :, :] = jnp.zeros((512, WIDTH), BF)

    def transposed(t):
        left = jnp.concatenate([merged[t + q, 4 - q] for q in range(5)], axis=0)
        right = dsc[pl.ds(pl.multiple_of(t * TILE, TILE), 5 * TILE), :]
        return lax.dot_general(left, right, TN, preferred_element_type=F32)

    for side, start in ((0, 0), (1, 18)):
        for i in range(2):
            rim_out[side, i * TILE : (i + 1) * TILE, :] = transposed(start + i).astype(BF)
    rim_low = remote(rim_out.at[0], rim_in.at[0], rim_s.at[0], rim_r.at[0], before)
    rim_high = remote(rim_out.at[1], rim_in.at[1], rim_s.at[1], rim_r.at[1], after)
    rim_low.start()
    rim_high.start()
    pending.extend((rim_low, rim_high))

    def interior(t, carry):
        here = rows_at(t * TILE, TILE)
        value = transposed(t + 2)
        value = value + lax.dot_general(dpre[here, :], ws[...], NT, preferred_element_type=F32)
        base[here, :] = value
        return carry

    lax.fori_loop(0, 8, interior, 0)
    g_x()
    lax.fori_loop(8, 16, interior, 0)
    hub_x_send()
    g_z()
    rim_low.wait_recv()
    rim_high.wait_recv()
    low = jnp.where(me == 0, 0.0, rim_in[1].astype(F32))
    base[:HALO, :] = base[:HALO, :] + low
    high = jnp.where(me == 127, 0.0, rim_in[0].astype(F32))
    base[ROWS - HALO :, :] = base[ROWS - HALO :, :] + high
    hub_y_send()
    g_gather_x()
    total = hub_total()
    g_gather_y()
    upper = total.astype(BF)
    lower = (total - upper.astype(F32)).astype(BF)
    right = jnp.concatenate([upper, lower, jnp.zeros((64, WIDTH), BF)], axis=0)

    def finish(j, carry):
        here = rows_at(j * 256, 256)
        ids = lax.broadcasted_iota(I32, (256, TILE), 0) + j * 256
        place = (ids == hub_row).astype(F32).astype(BF)
        value = base[here, :] + jnp.dot(place, right, preferred_element_type=F32)
        fgrad[here, :] = value.astype(BF)
        return carry

    lax.fori_loop(0, 8, finish, 0)
    store_g = pltpu.make_async_copy(fgrad, grad_hbm, store_sem.at[1])
    store_g.start()
    g_gather_core()
    for copy in pending:
        copy.wait_send()
    store_h.wait()
    store_g.wait()


SCRATCH = [
    VMEM((ROWS + 2 * HALO, WIDTH), BF),
    VMEM((TILES, SLOTS, TILE, TILE), I32),
    VMEM((ROWS, WIDTH), BF),
    VMEM((ROWS, WIDTH), BF),
    VMEM((ROWS, WIDTH), BF),
    VMEM((2, 4, 4, 4, 2, 32, TILE), BF),
    VMEM((HUBS, ROWS), BF),
    VMEM((4, ROWS), I32),
    VMEM((24, 5, TILE, TILE), BF),
    VMEM((ROWS, WIDTH), F32),
    VMEM((ROWS, WIDTH), F32),
    VMEM((ROWS, TILE), F32),
    VMEM((ROWS, WIDTH), BF),
    VMEM((ROWS, WIDTH), BF),
    VMEM((ROWS + 1024, WIDTH), BF),
    VMEM((512, WIDTH), F32),
    VMEM((ROWS, WIDTH), F32),
    VMEM((2, HALO, WIDTH), BF),
    VMEM((2, HALO, WIDTH), BF),
    VMEM((4, 4, 4, 2, 32, WIDTH), BF),
    VMEM((4, 4, 4, 32, WIDTH), BF),
    VMEM((3, 4, 4, 32, WIDTH), BF),
    VMEM((3, 4, 4, 32, WIDTH), BF),
    VMEM((4, 4, 32, WIDTH), F32),
    VMEM((4, 4, 32, WIDTH), BF),
    VMEM((3, 4, 32, WIDTH), BF),
    VMEM((4, 32, WIDTH), F32),
    VMEM((3, 32, WIDTH), F32),
    VMEM((2, 4, 4, 24, WIDTH), F32),
    VMEM((4, 4, 24, WIDTH), F32),
    VMEM((4, 4, 24, WIDTH), F32),
    VMEM((3, 4, 24, WIDTH), F32),
    VMEM((4, 24, WIDTH), F32),
    VMEM((3, 24, WIDTH), F32),
    VMEM((4, 24, WIDTH), F32),
    VMEM((2, 4, 4, 24, WIDTH), F32),
    DMA((2,)), DMA((TILES,)), DMA((2,)),
    DMA((2,)), DMA((2,)),
    DMA((3, 2, 3)), DMA((3, 2, 3)),
    DMA((8,)), DMA((8,)),
    DMA((2,)), DMA((2,)),
    DMA((4,)), DMA((4,)),
    DMA((3,)), DMA((3,)), DMA((3,)), DMA((3,)), DMA((3,)), DMA((3,)),
    DMA((1,)), DMA((1,)),
    DMA((3,)), DMA((3,)), DMA((3,)), DMA((3,)), DMA((3,)), DMA((3,)),
    DMA((3,)), DMA((3,)), DMA((3,)), DMA((3,)),
    DMA((1,)), DMA((1,)),
]


def local(
    features, self_weight, neighbor_weight, bias_term, tile_columns, tile_bits,
    hub_slots, hub_live, degree, hub_rows, cotangent,
):
    smem = pl.BlockSpec(memory_space=pltpu.SMEM)
    vmem = pl.BlockSpec(memory_space=VMEM)
    hbm = pl.BlockSpec(memory_space=pl.ANY)
    hidden, feature_grad, sums = pl.pallas_call(
        kernel,
        out_shape=(
            jax.ShapeDtypeStruct((ROWS, WIDTH), BF),
            jax.ShapeDtypeStruct((ROWS, WIDTH), BF),
            jax.ShapeDtypeStruct((520, WIDTH), F32),
        ),
        in_specs=[smem, smem, hbm, hbm, hbm] + [vmem] * 6,
        out_specs=(hbm, hbm, vmem),
        scratch_shapes=SCRATCH,
        name="sage_layer",
        compiler_params=pltpu.CompilerParams(
            collective_id=0, has_side_effects=True, vmem_limit_bytes=60 * 2**20
        ),
    )(
        tile_columns.T, hub_rows, features, tile_bits, cotangent, self_weight, neighbor_weight,
        bias_term.reshape(1, WIDTH), hub_slots.T, hub_live.T, degree.reshape(TILES, TILE),
    )
    return hidden, feature_grad, sums[:256], sums[256:512], sums[512]


def solution(mesh):
    placed = (
        P("band", None), P(), P(), P(), P("band", None), P("band", None, None, None),
        P("band", None), P("band", None), P("band"), P("band"), P("band", None),
    )
    return jax.shard_map(
        local,
        mesh=mesh,
        in_specs=placed,
        out_specs=(P("band", None), P("band", None), P(), P(), P()),
        check_vma=False,
    )
```

time: 339 us -> 83.3 us (0.25)
  waiting for transfers between devices: 116 us -> 0 us
  matrix products: 105 us -> 0 us
  Pallas kernels: 0 us -> 73.6 us
  blocking collectives: 66.5 us -> 0 us
  between operations: 14.4 us -> 0.65 us
  other arithmetic: 10.9 us -> 0 us
  starting transfers between devices: 10.9 us -> 0 us
  local copies, waits for them, and re-layouts: 14.2 us -> 7.63 us
    dot_general x27 -> x0, matrix products: 105 us -> none  [the longest x4 42.6 us: hub_backward(): jnp.einsum('nh,nf->hf', counts, grad_block, preferred_element_type=jnp.fl...]
    psum x1 -> x0, waiting for transfers between devices: 73.9 us -> none  [local(): hub_whole = lax.psum(hub_part, 'band')]
    pallas_call x0 -> x1, Pallas kernels: none -> 73.6 us  [local(): pl.pallas_call(kernel, out_shape=(jax.ShapeDtypeStruct((ROWS, WIDTH), BF)...]
    psum x1 -> x0, blocking collectives: 66.5 us -> none  [local(): lax.psum((self_part, neighbor_part, bias_part), 'band')]
    all_gather x1 -> x0, waiting for transfers between devices: 42.6 us -> none  [local(): hub_table = lax.all_gather(own_table, 'band', axis=0, tiled=True)]
    ppermute x4 -> x0, starting transfers between devices: 10.8 us -> none  [the longest x2 6.56 us: padded(): lax.ppermute(lax.slice_in_dim(block, block.shape[dim] - width, None, axis...]
    convert_element_type x3 -> x0, other arithmetic: 5.66 us -> none  [the longest x1 3.57 us: local(): tile_bits.astype(jnp.bfloat16)]
    slice x14 -> x2, local copies, waits for them, and re-layouts: 7.36 us -> 3.11 us  [local(): return (hidden, feature_grad, sums[:256], sums[256:512], sums[512])]
  transfers between devices with their start and end apart: 6 -> 0, of which waited for: 2 -> 0; matrix products, arithmetic and copies ran while one was open for 8% -> 0% of each run, Pallas kernels for 0% -> 0%
where the time goes in v1:
time: 83.3 us; the launch traced here: 81.9 us
  Pallas kernels  73.6 us (88%)
  local copies, waits for them, and re-layouts  7.63 us (9%)
    pallas_call x1, Pallas kernels, local(): pl.pallas_call(kernel, out_shape=(jax.ShapeDtypeStruct((ROWS, WIDTH), BF)...  73.6 us
    unnamed x2, local copies, waits for them, and re-layouts  4.52 us
    slice x2, local copies, waits for them, and re-layouts, local(): return (hidden, feature_grad, sums[:256], sums[256:512], sums[512])  3.11 us

profile of v1, /device:TPU:1, one launch (start us, length us, event | category | flops | bytes accessed | tf_op | source)
XLA Modules:
  0.0 81.9 jit_solution(1685886351569000646)
XLA Ops:
  0.6 73.6 %sage_layer.1 = (bf16[2048,256]{1,0:T(8,128)(2,1)}, bf16[2048,256]{1,0:T(8,128)(2,1)}, f32[520,256]{1,0:T(8,128)}) custom-call(s32[6,16]{1,0:T(8,128)} %bitcast.9, s32[32]{0:T(128)} %hrow.1, bf16[2048,256]{1,0:T(8,128)(2,1)} %feat_hbm.1, s32[16,6,128,128]{3,2,1,0:T(8,128)} %bits_hbm.1, bf16[2048,256]{1,0:T(8,128)(2,1)} %cot_hbm.1, bf16[256,256]{1,0:T(8,128)(2,1)} %ws.1, ...), custom_call_target="tpu_custom_call" | custom-call | tf_op jit(solution)/shard_map/sage_layer/pallas_call | solution.py:519
  74.3 1.9 %fusion = (f32[256,256]{1,0:T(8,128)}, f32[256,256]{1,0:T(8,128)}) fusion(f32[520,256]{1,0:T(8,128)} %get-tuple-element.10), kind=kLoop, calls=%fused_computation | loop fusion | bytes 1048576 | tf_op jit(solution)/shard_map/slice | solution.py:537
  76.1 1.3 %slice.11 = f32[1,256]{1,0:T(1,128)} slice(f32[520,256]{1,0:T(8,128)} %get-tuple-element.10), slice={[512:513], [0:256]} | slice | bytes 2048 | tf_op jit(solution)/shard_map/slice | solution.py:537
  77.4 2.3 %copy.18 = bf16[2048,256]{1,0:T(8,128)(2,1)} copy(bf16[2048,256]{1,0:T(8,128)(2,1)} %get-tuple-element.18) | data formatting | bytes 2097152
  79.6 2.3 %copy.19 = bf16[2048,256]{1,0:T(8,128)(2,1)} copy(bf16[2048,256]{1,0:T(8,128)(2,1)} %get-tuple-element.19) | data formatting | bytes 2097152

commit v2 on v1

v2 whole, which is shorter than its diff:
```python
import math

import jax
import jax.numpy as jnp
from jax import lax
from jax.experimental import pallas as pl
from jax.experimental.pallas import tpu as pltpu
from jax.sharding import PartitionSpec as P

MESH = pl.DeviceIdType.MESH
BF = jnp.bfloat16
F32 = jnp.float32
I32 = jnp.int32
VMEM = pltpu.VMEM
DMA = pltpu.SemaphoreType.DMA

ROWS = 2048
WIDTH = 256
TILE = 128
TILES = 16
SLOTS = 6
HALO = 256
HUBS = 4096
ORDERS = ((0, 1, 2), (1, 2, 0))
PLANE = [(i, j) for i in range(4) for j in range(4) if (i, j) != (0, 0)]
PLANE.sort(key=lambda step: -min(step[0], 4 - step[0]) - min(step[1], 4 - step[1]))
TN = (((0,), (0,)), ((), ()))
NT = (((1,), (1,)), ((), ()))


def device(z, x, y, c):
    return ((z * 4 + x) * 4 + y) * 2 + c


def rows_at(start, size):
    return pl.ds(pl.multiple_of(start, size), size)


def remote(src, dst, send, recv, target):
    return pltpu.make_async_remote_copy(
        src_ref=src, dst_ref=dst, send_sem=send, recv_sem=recv, device_id=(target,), device_id_type=MESH
    )


def kernel(
    tcol, hrow, feat_hbm, bits_hbm, cot_hbm, ws_hbm, wn_hbm, bias_hbm, slots_hbm, live_hbm, deg_hbm,
    hid, fgrad, sums,
    feat, low, high, bits, cot, ws, wn, bias, slots, live, deg, table, counts, slot_low, slot_high, onehot, merged, band, pre0,
    rdeg, agg, dpre, dsc, base, rim_out, rim_in,
    hubp, hubc, hubs, recv_a, sum_a, out_b, recv_b, sum_b, recv_c,
    gpart, gcore, gsum, gxy, gz, gall,
    load_sem, bits_sem, halo_s, halo_r, ag_s, ag_r, line_s, line_r, core_s, core_r, rim_s, rim_r,
    hc_s, hc_r, ha_s, ha_r, hb_s, hb_r, hd_s, hd_r,
    gc_s, gc_r, gxy_s, gxy_r, gz_s, gz_r, gg_s, gg_r, gh_s, gh_r,
):
    me = lax.axis_index("band")
    z, x, y, c = me // 32, (me // 8) % 4, (me // 2) % 4, me % 2
    at = (z, x, y)
    partner = device(z, x, y, 1 - c)
    after, before = (me + 1) % 128, (me + 127) % 128

    def peer(dim, k):
        place = list(at)
        place[dim] = (place[dim] + k) % 4
        return tuple(place)

    load_f = pltpu.make_async_copy(feat_hbm, feat, load_sem.at[0])
    load_f.start()
    small = [
        pltpu.make_async_copy(source, target, load_sem.at[2 + i])
        for i, (source, target) in enumerate(
            ((slots_hbm, slots), (live_hbm, live), (ws_hbm, ws), (wn_hbm, wn), (bias_hbm, bias), (deg_hbm, deg))
        )
    ]
    barrier = pltpu.get_barrier_semaphore()
    greeted = [partner, after, before]
    greeted.extend(device(*peer(0, k), c) for k in (1, 2, 3))
    greeted.extend(device(z, (x + i) % 4, (y + j) % 4, c) for i, j in PLANE)
    for other in greeted:
        pl.semaphore_signal(barrier, inc=1, device_id=(other,), device_id_type=MESH)
    for load in small:
        load.start()
    load_c = pltpu.make_async_copy(cot_hbm, cot, load_sem.at[1])
    bit_loads = []
    for r in range(TILES):
        load = pltpu.make_async_copy(bits_hbm.at[r], bits.at[r], bits_sem.at[r])
        load.start()
        bit_loads.append(load)
    load_c.start()

    lane = lax.broadcasted_iota(I32, (32, TILE), 1)
    sub = lax.broadcasted_iota(I32, (32, TILE), 0)
    hub_col = jnp.full((32, TILE), -1, I32)
    hub_row = jnp.full((1, TILE), -1, I32)
    lane1 = lax.broadcasted_iota(I32, (1, TILE), 1)
    for h in range(32):
        value = hrow[h]
        hub_col = jnp.where(sub == h, value, hub_col)
        hub_row = jnp.where((lane1 == h) | (lane1 == h + 32), value, hub_row)
    pick = jnp.concatenate(
        [(hub_col == lane + j * TILE).astype(F32).astype(BF) for j in range(TILES)], axis=1
    )
    load_f.wait()
    own = jnp.dot(pick, feat[...].reshape(ROWS, WIDTH), preferred_element_type=F32).astype(BF)
    table[0, z, x, y, c] = own[:, :TILE]
    table[1, z, x, y, c] = own[:, TILE:]

    pl.semaphore_wait(barrier, len(greeted))

    def line(half, place, core, free):
        index = [half] + [slice(None) if d in free else place[d] for d in range(3)] + [core]
        return table.at[tuple(index)]

    pending = []

    def gather_send(phase, half):
        dim, free = ORDERS[half][phase], ORDERS[half][:phase]
        block = line(half, at, c, free)
        for k in (1, 3, 2):
            copy = remote(block, block, ag_s.at[phase, half, k - 1], ag_r.at[phase, half, k - 1], device(*peer(dim, k), c))
            copy.start()
            pending.append(copy)

    def gather_recv(phase, half, k):
        dim, free = ORDERS[half][phase], ORDERS[half][:phase]
        block = line(half, peer(dim, 4 - k), c, free)
        remote(block, block, ag_s.at[phase, half, k - 1], ag_r.at[phase, half, k - 1], device(*peer(dim, k), c)).wait_recv()

    def line_send(half, k):
        middle, last = ORDERS[half][1:]
        block = line(half, peer(middle, (4 - k) % 4), c, ORDERS[half][:1])
        for i in (1, 3, 2):
            copy = remote(block, block, line_s.at[half, k, i - 1], line_r.at[half, k, i - 1], device(*peer(last, i), c))
            copy.start()
            pending.append(copy)

    def line_recv(half, i):
        middle, last = ORDERS[half][1:]
        place = list(peer(last, 4 - i))
        for k in range(4):
            piece = list(place)
            piece[middle] = (piece[middle] + 4 - k) % 4
            block = line(half, piece, c, ORDERS[half][:1])
            remote(block, block, line_s.at[half, k, i - 1], line_r.at[half, k, i - 1], partner).wait_recv()
        return line(half, place, c, ORDERS[half][:2])

    def core_send(block, n):
        copy = remote(block, block, core_s.at[n], core_r.at[n], partner)
        copy.start()
        pending.append(copy)

    def core_recv(half, place, n):
        block = line(half, place, 1 - c, ORDERS[half][:2])
        remote(block, block, core_s.at[n], core_r.at[n], partner).wait_recv()

    gather_send(0, 0)
    gather_send(0, 1)

    for load in small:
        load.wait()
    named = jnp.where(live[...] == 1, slots[...], -1)
    slot_low[...] = named & 255
    slot_high[...] = named >> 8
    span = 512

    def build(j, carry):
        cols = rows_at(j * span, span)
        ids = lax.broadcasted_iota(I32, (256, span), 0).astype(jnp.int16)
        for k in range(4):
            value = jnp.broadcast_to(slot_low[k : k + 1, cols], (16, span)).astype(jnp.int16)
            value = jnp.broadcast_to(value[None], (16, 16, span)).reshape(256, span)
            onehot[k] = jnp.where(value == ids, jnp.ones((), BF), jnp.zeros((), BF))

        def block(h, carry):
            total = jnp.zeros((256, span), BF)
            for k in range(4):
                keep = jnp.broadcast_to(jnp.where(slot_high[k : k + 1, cols] == h, 1.0, 0.0), (16, span)).astype(BF)
                keep = jnp.broadcast_to(keep[None], (16, 16, span)).reshape(256, span)
                total = total + onehot[k] * keep
            counts[rows_at(h * 256, 256), cols] = total
            return carry

        return lax.fori_loop(0, HUBS // 256, block, carry)

    lax.fori_loop(0, 2, build, 0)
    for half in range(2):
        for k in (1, 3, 2):
            gather_recv(0, half, k)
        gather_send(1, half)
        line_send(half, 0)
    lax.fori_loop(2, 4, build, 0)
    for k in (1, 3, 2):
        for half in range(2):
            gather_recv(1, half, k)
            line_send(half, k)
    halo_low = remote(feat.at[0:2], high.at[4:6], halo_s.at[0], halo_r.at[0], before)
    halo_high = remote(feat.at[14:16], low.at[0:2], halo_s.at[1], halo_r.at[1], after)
    halo_low.start()
    halo_high.start()
    pending.extend((halo_low, halo_high))
    for half in range(2):
        core_send(line(half, at, c, ORDERS[half][:2]), half)

    def own_term(j, carry):
        here = rows_at(j * 256, 256)
        pre0[here, :] = jnp.dot(feat[pl.ds(j * 2, 2)].reshape(256, WIDTH), ws[...], preferred_element_type=F32) + bias[...]
        return carry

    def divide(r, carry):
        row = 1.0 / deg[pl.ds(r, 1), :].astype(F32)
        rdeg[rows_at(r * TILE, TILE), :] = jnp.broadcast_to(row, (TILE, TILE)).T
        return carry

    def forward(rows, first):
        def body(r, carry):
            pltpu.make_async_copy(bits_hbm.at[r], bits.at[r], bits_sem.at[r]).wait()
            left = jnp.concatenate([bits[r, k].astype(F32).astype(BF) for k in range(SLOTS)], axis=1)
            right = jnp.concatenate([rows[jnp.clip(tcol[k, r] - first, 0, rows.shape[0] - 1)] for k in range(SLOTS)], axis=0)
            band[rows_at(r * TILE, TILE), :] = jnp.dot(left, right, preferred_element_type=F32)
            return carry

        return body

    lax.fori_loop(0, 8, own_term, 0)
    lax.fori_loop(0, TILES, divide, 0)
    lax.fori_loop(2, 8, forward(feat, 2), 0)
    n = 2
    for k in (1, 3):
        for half in range(2):
            core_send(line_recv(half, k), n)
            n += 1
    lax.fori_loop(8, 14, forward(feat, 2), 0)
    for half in range(2):
        core_send(line_recv(half, 2), n)
        n += 1
    low[2:6] = feat[0:4]
    high[0:4] = feat[12:16]
    halo_low.wait_recv()
    halo_high.wait_recv()
    low[0:2] = jnp.where(me == 0, 0.0, low[0:2].astype(F32)).astype(BF)
    high[4:6] = jnp.where(me == 127, 0.0, high[4:6].astype(F32)).astype(BF)
    lax.fori_loop(0, 2, forward(low, 0), 0)
    lax.fori_loop(14, 16, forward(high, 14), 0)

    n = 0
    for k in (0, 1, 3, 2):
        for half in range(2):
            core_recv(half, peer(ORDERS[half][2], (4 - k) % 4), n)
            n += 1

    load_c.wait()

    def layer(j, carry):
        cols = rows_at(j * 1024, 1024)
        right = jnp.concatenate([table[0].reshape(HUBS, TILE), table[1].reshape(HUBS, TILE)], axis=1)
        base[cols, :] = lax.dot_general(counts[:, cols], right, TN, preferred_element_type=F32)

        def chunk(i, carry):
            start = j * 1024 + i * 256
            here = rows_at(start, 256)
            for s in range(4):
                part = rows_at(start + s * 64, 64)
                scale = rdeg[part, :]
                total = band[part, :] + base[part, :]
                agg[part, :] = (total * jnp.concatenate([scale, scale], axis=1)).astype(BF)
            pre = pre0[here, :] + jnp.dot(agg[here, :], wn[...], preferred_element_type=F32)
            for s in range(4):
                part = rows_at(start + s * 64, 64)
                v = pre[s * 64 : s * 64 + 64, :]
                sig = 1.0 / (1.0 + jnp.exp(-v))
                act = v * sig
                hid[part, :] = act.astype(BF)
                dpre[part, :] = (cot[part, :].astype(F32) * sig * (1.0 + v - act)).astype(BF)
            back = lax.dot_general(dpre[here, :], wn[...], NT, preferred_element_type=F32)
            scale = rdeg[here, :]
            dsc[rows_at(512 + start, 256), :] = (back * jnp.concatenate([scale, scale], axis=1)).astype(BF)
            return carry

        return lax.fori_loop(0, 4, chunk, carry)

    lax.fori_loop(0, 2, layer, 0)

    gpart[:, :, :, 32:40, :] = jnp.zeros((2, 4, 4, 8, TILE), F32)
    for which, left in ((0, feat[...].reshape(ROWS, WIDTH)), (1, agg[...])):
        part = lax.dot_general(left, dpre[...], TN, preferred_element_type=F32).reshape(4, 4, 16, WIDTH)
        gpart[which, :, :, 0:16, :] = part[..., :TILE]
        gpart[which, :, :, 16:32, :] = part[..., TILE:]
    part = jnp.dot(jnp.ones((16, ROWS), BF), dpre[...], preferred_element_type=F32)
    row8 = lax.broadcasted_iota(I32, (8, TILE), 0)
    gpart[0, 0, 0, 32:40, :] = jnp.where(row8 == 0, part[:8, :TILE], jnp.where(row8 == 1, part[:8, TILE:], 0.0))
    copy_gc = remote(gpart.at[1 - c], gcore, gc_s.at[0], gc_r.at[0], partner)
    copy_gc.start()
    pending.append(copy_gc)

    def g_core():
        copy_gc.wait_recv()
        gsum[...] = gpart[c] + gcore[...]
        for n, (i, j) in enumerate(PLANE):
            there = ((x + i) % 4, (y + j) % 4)
            copy = remote(gsum.at[there[1], there[0]], gxy.at[n], gxy_s.at[n], gxy_r.at[n], device(z, *there, c))
            copy.start()
            pending.append(copy)

    def g_plane():
        total = gsum[y, x]
        for n in range(15):
            remote(gsum.at[y, x], gxy.at[n], gxy_s.at[n], gxy_r.at[n], partner).wait_recv()
            total = total + gxy[n]
        gz[z] = total
        for k in (1, 3, 2):
            copy = remote(gz.at[z], gz.at[z], gz_s.at[k - 1], gz_r.at[k - 1], device(*peer(0, k), c))
            copy.start()
            pending.append(copy)

    def g_z():
        for k in (1, 2, 3):
            slot = gz.at[(z + 4 - k) % 4]
            remote(slot, slot, gz_s.at[k - 1], gz_r.at[k - 1], partner).wait_recv()
        gall[c, y, x] = (gz[0] + gz[1] + gz[2] + gz[3]) * (1.0 / 512.0)
        piece = gall.at[c, y, x]
        for n, (i, j) in enumerate(PLANE):
            copy = remote(piece, piece, gg_s.at[n], gg_r.at[n], device(z, (x + i) % 4, (y + j) % 4, c))
            copy.start()
            pending.append(copy)

    def g_gather():
        for n, (i, j) in enumerate(PLANE):
            slot = gall.at[c, (y + 4 - j) % 4, (x + 4 - i) % 4]
            remote(slot, slot, gg_s.at[n], gg_r.at[n], partner).wait_recv()
        piece = gall.at[c]
        copy = remote(piece, piece, gh_s.at[0], gh_r.at[0], partner)
        copy.start()
        pending.append(copy)

    def g_done():
        slot = gall.at[1 - c]
        remote(slot, slot, gh_s.at[0], gh_r.at[0], partner).wait_recv()

    def hub_part(zc):
        left = counts[rows_at(zc * 1024, 1024), :]
        value = jnp.dot(left, dsc[512 : 512 + ROWS, :], preferred_element_type=F32)
        hubp[zc] = value.astype(BF).reshape(4, 4, 2, 32, WIDTH)
        copy = remote(hubp.at[zc, :, :, 1 - c], hubc.at[zc], hc_s.at[zc], hc_r.at[zc], partner)
        copy.start()
        pending.append(copy)

    def hub_add(zc):
        remote(hubp.at[zc, :, :, 1 - c], hubc.at[zc], hc_s.at[zc], hc_r.at[zc], partner).wait_recv()
        for i in range(4):
            total = (hubp[zc, i, :, c].astype(F32) + hubc[zc, i].astype(F32)).astype(BF)
            hubs[0, zc, i] = total[..., :TILE]
            hubs[1, zc, i] = total[..., TILE:]

    def send_a(zc):
        for k in (2, 1, 3):
            for half in range(2):
                source = hubs.at[0, zc, (x + k) % 4] if half == 0 else hubs.at[1, zc, :, (y + k) % 4]
                copy = remote(
                    source, recv_a.at[half, k - 1, zc], ha_s.at[half, k - 1, zc], ha_r.at[half, k - 1, zc],
                    device(*peer(1 + half, k), c),
                )
                copy.start()
                pending.append(copy)

    def collect(zc):
        for k in range(3):
            for half in range(2):
                block = recv_a.at[half, k, zc]
                remote(block, block, ha_s.at[half, k, zc], ha_r.at[half, k, zc], partner).wait_recv()
        totals = []
        for half in range(2):
            total = (hubs[0, zc, x] if half == 0 else hubs[1, zc, :, y]).astype(F32)
            for k in range(3):
                total = total + recv_a[half, k, zc].astype(F32)
            totals.append(total)
        return totals

    def send_b(k):
        for half, total in enumerate(collect((z + k) % 4)):
            out_b[k - 1, half] = total.astype(BF)
        copy = remote(out_b.at[k - 1], recv_b.at[k - 1], hb_s.at[k - 1], hb_r.at[k - 1], device(*peer(0, k), c))
        copy.start()
        pending.append(copy)

    def send_c():
        for k in range(3):
            remote(recv_b.at[k], recv_b.at[k], hb_s.at[k], hb_r.at[k], partner).wait_recv()
        for half in range(2):
            total = sum_a[half]
            for k in range(3):
                total = total + recv_b[k, half].astype(F32)
            sum_b[half] = total
        for k in (2, 1, 3):
            for half, dim in ((0, 2), (1, 1)):
                copy = remote(
                    sum_b.at[half, (at[dim] + k) % 4], recv_c.at[half, k - 1],
                    hd_s.at[half, k - 1], hd_r.at[half, k - 1], device(*peer(dim, k), c),
                )
                copy.start()
                pending.append(copy)

    def hub_total(half):
        for k in range(3):
            remote(recv_c.at[half, k], recv_c.at[half, k], hd_s.at[half, k], hd_r.at[half, k], partner).wait_recv()
        return sum_b[half, at[2 - half]] + recv_c[half, 0] + recv_c[half, 1] + recv_c[half, 2]

    def merge(r, carry):
        weight = [[(tcol[k, r] == r + o).astype(F32) for k in range(SLOTS)] for o in range(5)]
        for s in range(4):
            part = pl.ds(s * 32, 32)
            total = [jnp.zeros((32, TILE), F32) for _ in range(5)]
            for k in range(SLOTS):
                value = bits[r, k, part, :].astype(F32)
                for o in range(5):
                    total[o] = total[o] + value * weight[o][k]
            for o in range(5):
                merged[r + 4, o, part, :] = total[o].astype(BF)
        return carry

    hub_part((z + 2) % 4)
    hub_part((z + 1) % 4)
    g_core()
    hub_part((z + 3) % 4)
    hub_add((z + 2) % 4)
    send_a((z + 2) % 4)
    hub_part(z)
    hub_add((z + 1) % 4)
    send_a((z + 1) % 4)
    merged[0:4] = jnp.zeros((4, 5, TILE, TILE), BF)
    merged[20:24] = jnp.zeros((4, 5, TILE, TILE), BF)
    hub_add((z + 3) % 4)
    send_a((z + 3) % 4)
    lax.fori_loop(0, 4, merge, 0)
    hub_add(z)
    send_a(z)
    send_b(2)
    g_plane()
    lax.fori_loop(4, 8, merge, 0)
    send_b(1)
    lax.fori_loop(8, 12, merge, 0)
    send_b(3)
    g_z()
    lax.fori_loop(12, 16, merge, 0)
    for half, total in enumerate(collect(z)):
        sum_a[half] = total

    dsc[0:512, :] = jnp.zeros((512, WIDTH), BF)
    dsc[512 + ROWS :, :] = jnp.zeros((512, WIDTH), BF)

    def transposed(t):
        left = jnp.concatenate([merged[t + q, 4 - q] for q in range(5)], axis=0)
        right = dsc[pl.ds(pl.multiple_of(t * TILE, TILE), 5 * TILE), :]
        return lax.dot_general(left, right, TN, preferred_element_type=F32)

    for side, start in ((0, 0), (1, 18)):
        for i in range(2):
            rim_out[side, i * TILE : (i + 1) * TILE, :] = transposed(start + i).astype(BF)
    rim_low = remote(rim_out.at[0], rim_in.at[0], rim_s.at[0], rim_r.at[0], before)
    rim_high = remote(rim_out.at[1], rim_in.at[1], rim_s.at[1], rim_r.at[1], after)
    rim_low.start()
    rim_high.start()
    pending.extend((rim_low, rim_high))

    def interior(t, carry):
        here = rows_at(t * TILE, TILE)
        value = transposed(t + 2)
        value = value + lax.dot_general(dpre[here, :], ws[...], NT, preferred_element_type=F32)
        base[here, :] = value
        return carry

    lax.fori_loop(0, 4, interior, 0)
    send_c()
    lax.fori_loop(4, 16, interior, 0)
    g_gather()
    rim_low.wait_recv()
    rim_high.wait_recv()
    low = jnp.where(me == 0, 0.0, rim_in[1].astype(F32))
    base[:HALO, :] = base[:HALO, :] + low
    high = jnp.where(me == 127, 0.0, rim_in[0].astype(F32))
    base[ROWS - HALO :, :] = base[ROWS - HALO :, :] + high
    total = jnp.concatenate([hub_total(0), hub_total(1)], axis=1)
    upper = total.astype(BF)
    lower = (total - upper.astype(F32)).astype(BF)
    right = jnp.concatenate([upper, lower, jnp.zeros((64, WIDTH), BF)], axis=0)

    def finish(j, carry):
        here = rows_at(j * 256, 256)
        ids = lax.broadcasted_iota(I32, (256, TILE), 0) + j * 256
        place = (ids == hub_row).astype(F32).astype(BF)
        value = base[here, :] + jnp.dot(place, right, preferred_element_type=F32)
        fgrad[here, :] = value.astype(BF)
        return carry

    lax.fori_loop(0, 8, finish, 0)
    g_done()
    sums[...] = gall[...]
    for copy in pending:
        copy.wait_send()


def deliver(hid, fgrad, gall, hidden_out, grad_out, self_out, neighbor_out, bias_out, sem):
    copies = [pltpu.make_async_copy(hid, hidden_out, sem.at[0]), pltpu.make_async_copy(fgrad, grad_out, sem.at[1])]
    for copy in copies:
        copy.start()
    for which, out in ((0, self_out), (1, neighbor_out)):
        out[:, :TILE] = gall[which, :, :, 0:16, :].reshape(WIDTH, TILE)
        out[:, TILE:] = gall[which, :, :, 16:32, :].reshape(WIDTH, TILE)
    bias_out[:, :TILE] = gall[0, 0, 0, 32:33, :]
    bias_out[:, TILE:] = gall[0, 0, 0, 33:34, :]
    for copy in copies:
        copy.wait()


SCRATCH = [
    VMEM((TILES, TILE, WIDTH), BF),
    VMEM((6, TILE, WIDTH), BF),
    VMEM((6, TILE, WIDTH), BF),
    VMEM((TILES, SLOTS, TILE, TILE), I32),
    VMEM((ROWS, WIDTH), BF),
    VMEM((WIDTH, WIDTH), BF),
    VMEM((WIDTH, WIDTH), BF),
    VMEM((1, WIDTH), F32),
    VMEM((4, ROWS), I32),
    VMEM((4, ROWS), I32),
    VMEM((TILES, TILE), I32),
    VMEM((2, 4, 4, 4, 2, 32, TILE), BF),
    VMEM((HUBS, ROWS), BF),
    VMEM((4, ROWS), I32),
    VMEM((4, ROWS), I32),
    VMEM((4, 256, 512), BF),
    VMEM((24, 5, TILE, TILE), BF),
    VMEM((ROWS, WIDTH), F32),
    VMEM((ROWS, WIDTH), F32),
    VMEM((ROWS, TILE), F32),
    VMEM((ROWS, WIDTH), BF),
    VMEM((ROWS, WIDTH), BF),
    VMEM((ROWS + 1024, WIDTH), BF),
    VMEM((ROWS, WIDTH), F32),
    VMEM((2, HALO, WIDTH), BF),
    VMEM((2, HALO, WIDTH), BF),
    VMEM((4, 4, 4, 2, 32, WIDTH), BF),
    VMEM((4, 4, 4, 32, WIDTH), BF),
    VMEM((2, 4, 4, 4, 32, TILE), BF),
    VMEM((2, 3, 4, 4, 32, TILE), BF),
    VMEM((2, 4, 32, TILE), F32),
    VMEM((3, 2, 4, 32, TILE), BF),
    VMEM((3, 2, 4, 32, TILE), BF),
    VMEM((2, 4, 32, TILE), F32),
    VMEM((2, 3, 32, TILE), F32),
    VMEM((2, 4, 4, 40, TILE), F32),
    VMEM((4, 4, 40, TILE), F32),
    VMEM((4, 4, 40, TILE), F32),
    VMEM((15, 40, TILE), F32),
    VMEM((4, 40, TILE), F32),
    VMEM((2, 4, 4, 40, TILE), F32),
    DMA((8,)), DMA((TILES,)),
    DMA((2,)), DMA((2,)),
    DMA((2, 2, 3)), DMA((2, 2, 3)),
    DMA((2, 4, 3)), DMA((2, 4, 3)),
    DMA((8,)), DMA((8,)),
    DMA((2,)), DMA((2,)),
    DMA((4,)), DMA((4,)),
    DMA((2, 3, 4)), DMA((2, 3, 4)), DMA((3,)), DMA((3,)), DMA((2, 3)), DMA((2, 3)),
    DMA((1,)), DMA((1,)),
    DMA((15,)), DMA((15,)),
    DMA((3,)), DMA((3,)),
    DMA((15,)), DMA((15,)),
    DMA((1,)), DMA((1,)),
]


def local(
    features, self_weight, neighbor_weight, bias_term, tile_columns, tile_bits,
    hub_slots, hub_live, degree, hub_rows, cotangent,
):
    smem = pl.BlockSpec(memory_space=pltpu.SMEM)
    vmem = pl.BlockSpec(memory_space=VMEM)
    hbm = pl.BlockSpec(memory_space=pl.ANY)
    wide = jax.ShapeDtypeStruct((ROWS, WIDTH), BF)
    hidden, feature_grad, sums = pl.pallas_call(
        kernel,
        out_shape=(VMEM(wide.shape, BF), VMEM(wide.shape, BF), VMEM((2, 4, 4, 40, TILE), F32)),
        in_specs=[smem, smem] + [hbm] * 9,
        out_specs=(vmem, vmem, vmem),
        scratch_shapes=SCRATCH,
        name="sage_layer",
        compiler_params=pltpu.CompilerParams(
            collective_id=0, has_side_effects=True, vmem_limit_bytes=56 * 2**20
        ),
    )(
        tile_columns.T, hub_rows, features.reshape(TILES, TILE, WIDTH), tile_bits, cotangent, self_weight, neighbor_weight,
        bias_term.reshape(1, WIDTH), hub_slots.T, hub_live.T, degree.reshape(TILES, TILE),
    )
    square = jax.ShapeDtypeStruct((WIDTH, WIDTH), F32)
    hidden, feature_grad, self_grad, neighbor_grad, bias_grad = pl.pallas_call(
        deliver,
        out_shape=(wide, wide, square, square, jax.ShapeDtypeStruct((1, WIDTH), F32)),
        in_specs=[vmem, vmem, vmem],
        out_specs=(hbm, hbm, vmem, vmem, vmem),
        scratch_shapes=[DMA((2,))],
        compiler_params=pltpu.CompilerParams(vmem_limit_bytes=8 * 2**20),
        name="deliver",
    )(*(pltpu.with_memory_space_constraint(value, VMEM) for value in (hidden, feature_grad, sums)))
    return hidden, feature_grad, self_grad, neighbor_grad, bias_grad.reshape(WIDTH)


def solution(mesh):
    placed = (
        P("band", None), P(), P(), P(), P("band", None), P("band", None, None, None),
        P("band", None), P("band", None), P("band"), P("band"), P("band", None),
    )
    return jax.shard_map(
        local,
        mesh=mesh,
        in_specs=placed,
        out_specs=(P("band", None), P("band", None), P(), P(), P()),
        check_vma=False,
    )
```

time: 83.3 us -> 68.7 us (0.82)
  local copies, waits for them, and re-layouts: 7.63 us -> 0 us
  Pallas kernels: 73.6 us -> 67.1 us
    pallas_call x1 -> x2, Pallas kernels: 73.6 us -> 67.1 us  [the longest x1 64.9 us: local(): pl.pallas_call(kernel, out_shape=(VMEM(wide.shape, BF), VMEM(wide.shape,...]
    unnamed x2 -> x0, local copies, waits for them, and re-layouts: 4.52 us -> none
    slice x2 -> x0, local copies, waits for them, and re-layouts: 3.11 us -> none  [local(): return (hidden, feature_grad, sums[:256], sums[256:512], sums[512])]
where the time goes in v2:
time: 68.7 us; the launch traced here: 67.7 us
  Pallas kernels  67.1 us (98%)
    pallas_call x1, Pallas kernels, local(): pl.pallas_call(kernel, out_shape=(VMEM(wide.shape, BF), VMEM(wide.shape,...  64.9 us
    pallas_call x1, Pallas kernels, local(): pl.pallas_call(deliver, out_shape=(wide, wide, square, square, jax.ShapeD...  2.12 us

profile of v2, /device:TPU:1, one launch (start us, length us, event | category | flops | bytes accessed | tf_op | source)
XLA Modules:
  0.0 67.7 jit_solution(6660759099003799108)
XLA Ops:
  0.6 64.9 %sage_layer.1 = (bf16[2048,256]{1,0:T(8,128)(2,1)S(1)}, bf16[2048,256]{1,0:T(8,128)(2,1)S(1)}, f32[2,4,4,40,128]{4,3,2,1,0:T(8,128)S(1)}) custom-call(s32[6,16]{1,0:T(8,128)} %bitcast.11, s32[32]{0:T(128)} %hrow.1, bf16[16,128,256]{2,1,0:T(8,128)(2,1)} %bitcast.7, s32[16,6,128,128]{3,2,1,0:T(8,128)} %bits_hbm.1, bf16[2048,256]{1,0:T(8,128)(2,1)} %cot_hbm.1, ...), custom_call_target="tpu_custom_call" | custom-call | tf_op jit(solution)/shard_map/sage_layer/pallas_call | solution.py:580
  65.6 2.1 %deliver.1 = (bf16[2048,256]{1,0:T(8,128)(2,1)}, bf16[2048,256]{1,0:T(8,128)(2,1)}, f32[256,256]{1,0:T(8,128)}, f32[256,256]{1,0:T(8,128)}, f32[1,256]{1,0:T(1,128)}) custom-call(bf16[2048,256]{1,0:T(8,128)(2,1)S(1)} %get-tuple-element.13.hid, bf16[2048,256]{1,0:T(8,128)(2,1)S(1)} %get-tuple-element.14.fgrad, f32[2,4,4,40,128]{4,3,2,1,0:T(8,128)S(1)} %get-tuple-element.15.gall), custom_call_target="tpu_custom_call" | custom-call | tf_op jit(solution)/shard_map/deliver/pallas_call | solution.py:595

commit v3 on v2

--- a/solution.py
+++ b/solution.py
@@ -23,7 +23,6 @@
 HUBS = 4096
 ORDERS = ((0, 1, 2), (1, 2, 0))
 PLANE = [(i, j) for i in range(4) for j in range(4) if (i, j) != (0, 0)]
-PLANE.sort(key=lambda step: -min(step[0], 4 - step[0]) - min(step[1], 4 - step[1]))
 TN = (((0,), (0,)), ((), ()))
 NT = (((1,), (1,)), ((), ()))
 
@@ -48,7 +47,7 @@
     feat, low, high, bits, cot, ws, wn, bias, slots, live, deg, table, counts, slot_low, slot_high, onehot, merged, band, pre0,
     rdeg, agg, dpre, dsc, base, rim_out, rim_in,
     hubp, hubc, hubs, recv_a, sum_a, out_b, recv_b, sum_b, recv_c,
-    gpart, gcore, gsum, gxy, gz, gall,
+    gpart, gcore, gsum, gsend, gxy, gz, gall,
     load_sem, bits_sem, halo_s, halo_r, ag_s, ag_r, line_s, line_r, core_s, core_r, rim_s, rim_r,
     hc_s, hc_r, ha_s, ha_r, hb_s, hb_r, hd_s, hd_r,
     gc_s, gc_r, gxy_s, gxy_r, gz_s, gz_r, gg_s, gg_r, gh_s, gh_r,
@@ -248,6 +247,8 @@
             core_recv(half, peer(ORDERS[half][2], (4 - k) % 4), n)
             n += 1
 
+    early = len(pending)
+
     load_c.wait()
 
     def layer(j, carry):
@@ -292,21 +293,28 @@
     copy_gc.start()
     pending.append(copy_gc)
 
+    def plane(n):
+        return (x + n // 4) % 4, (y + n % 4) % 4
+
     def g_core():
         copy_gc.wait_recv()
-        gsum[...] = gpart[c] + gcore[...]
-        for n, (i, j) in enumerate(PLANE):
-            there = ((x + i) % 4, (y + j) % 4)
-            copy = remote(gsum.at[there[1], there[0]], gxy.at[n], gxy_s.at[n], gxy_r.at[n], device(z, *there, c))
-            copy.start()
-            pending.append(copy)
+        total = gpart[c] + gcore[...]
+        gsum[...] = total
+        gsend[...] = jnp.concatenate([total, jnp.zeros((4, 4, 8, TILE), F32)], axis=2).astype(BF)
+
+        def send(n, carry):
+            px, py = plane(n)
+            remote(gsend.at[py, px], gxy.at[n], gxy_s.at[n], gxy_r.at[n], device(z, px, py, c)).start()
+            return carry
+
+        lax.fori_loop(1, 16, send, 0)
 
     def g_plane():
-        total = gsum[y, x]
-        for n in range(15):
-            remote(gsum.at[y, x], gxy.at[n], gxy_s.at[n], gxy_r.at[n], partner).wait_recv()
-            total = total + gxy[n]
-        gz[z] = total
+        def add(n, total):
+            remote(gsend.at[y, x], gxy.at[n], gxy_s.at[n], gxy_r.at[n], partner).wait_recv()
+            return total + gxy[n, 0:40, :].astype(F32)
+
+        gz[z] = lax.fori_loop(1, 16, add, gsum[y, x])
         for k in (1, 3, 2):
             copy = remote(gz.at[z], gz.at[z], gz_s.at[k - 1], gz_r.at[k - 1], device(*peer(0, k), c))
             copy.start()
@@ -316,17 +324,24 @@
         for k in (1, 2, 3):
             slot = gz.at[(z + 4 - k) % 4]
             remote(slot, slot, gz_s.at[k - 1], gz_r.at[k - 1], partner).wait_recv()
-        gall[c, y, x] = (gz[0] + gz[1] + gz[2] + gz[3]) * (1.0 / 512.0)
+        total = (gz[0] + gz[1] + gz[2] + gz[3]) * (1.0 / 512.0)
+        gall[c, y, x] = jnp.concatenate([total, jnp.zeros((8, TILE), F32)], axis=0).astype(BF)
         piece = gall.at[c, y, x]
-        for n, (i, j) in enumerate(PLANE):
-            copy = remote(piece, piece, gg_s.at[n], gg_r.at[n], device(z, (x + i) % 4, (y + j) % 4, c))
-            copy.start()
-            pending.append(copy)
+
+        def send(n, carry):
+            px, py = plane(n)
+            remote(piece, piece, gg_s.at[n], gg_r.at[n], device(z, px, py, c)).start()
+            return carry
+
+        lax.fori_loop(1, 16, send, 0)
 
     def g_gather():
-        for n, (i, j) in enumerate(PLANE):
-            slot = gall.at[c, (y + 4 - j) % 4, (x + 4 - i) % 4]
+        def wait(n, carry):
+            slot = gall.at[c, (y + 4 - n % 4) % 4, (x + 4 - n // 4) % 4]
             remote(slot, slot, gg_s.at[n], gg_r.at[n], partner).wait_recv()
+            return carry
+
+        lax.fori_loop(1, 16, wait, 0)
         piece = gall.at[c]
         copy = remote(piece, piece, gh_s.at[0], gh_r.at[0], partner)
         copy.start()
@@ -340,9 +355,7 @@
         left = counts[rows_at(zc * 1024, 1024), :]
         value = jnp.dot(left, dsc[512 : 512 + ROWS, :], preferred_element_type=F32)
         hubp[zc] = value.astype(BF).reshape(4, 4, 2, 32, WIDTH)
-        copy = remote(hubp.at[zc, :, :, 1 - c], hubc.at[zc], hc_s.at[zc], hc_r.at[zc], partner)
-        copy.start()
-        pending.append(copy)
+        remote(hubp.at[zc, :, :, 1 - c], hubc.at[zc], hc_s.at[zc], hc_r.at[zc], partner).start()
 
     def hub_add(zc):
         remote(hubp.at[zc, :, :, 1 - c], hubc.at[zc], hc_s.at[zc], hc_r.at[zc], partner).wait_recv()
@@ -355,12 +368,10 @@
         for k in (2, 1, 3):
             for half in range(2):
                 source = hubs.at[0, zc, (x + k) % 4] if half == 0 else hubs.at[1, zc, :, (y + k) % 4]
-                copy = remote(
+                remote(
                     source, recv_a.at[half, k - 1, zc], ha_s.at[half, k - 1, zc], ha_r.at[half, k - 1, zc],
                     device(*peer(1 + half, k), c),
-                )
-                copy.start()
-                pending.append(copy)
+                ).start()
 
     def collect(zc):
         for k in range(3):
@@ -378,9 +389,7 @@
     def send_b(k):
         for half, total in enumerate(collect((z + k) % 4)):
             out_b[k - 1, half] = total.astype(BF)
-        copy = remote(out_b.at[k - 1], recv_b.at[k - 1], hb_s.at[k - 1], hb_r.at[k - 1], device(*peer(0, k), c))
-        copy.start()
-        pending.append(copy)
+        remote(out_b.at[k - 1], recv_b.at[k - 1], hb_s.at[k - 1], hb_r.at[k - 1], device(*peer(0, k), c)).start()
 
     def send_c():
         for k in range(3):
@@ -417,30 +426,44 @@
                 merged[r + 4, o, part, :] = total[o].astype(BF)
         return carry
 
-    hub_part((z + 2) % 4)
-    hub_part((z + 1) % 4)
-    g_core()
-    hub_part((z + 3) % 4)
-    hub_add((z + 2) % 4)
-    send_a((z + 2) % 4)
-    hub_part(z)
-    hub_add((z + 1) % 4)
-    send_a((z + 1) % 4)
+    def order(i):
+        return jnp.where(i == 0, 2, jnp.where(i == 1, 1, jnp.where(i == 2, 3, 0)))
+
     merged[0:4] = jnp.zeros((4, 5, TILE, TILE), BF)
     merged[20:24] = jnp.zeros((4, 5, TILE, TILE), BF)
-    hub_add((z + 3) % 4)
-    send_a((z + 3) % 4)
-    lax.fori_loop(0, 4, merge, 0)
-    hub_add(z)
-    send_a(z)
-    send_b(2)
+
+    def step(i, carry):
+        @pl.when(i < 4)
+        def _():
+            hub_part((z + order(i)) % 4)
+
+        @pl.when(i == 1)
+        def _():
+            g_core()
+
+        @pl.when(i >= 4)
+        def _():
+            lax.fori_loop((i - 4) * 4, (i - 3) * 4, merge, 0)
+
+        @pl.when(i >= 2)
+        def _():
+            zc = (z + order(i - 2)) % 4
+            hub_add(zc)
+            send_a(zc)
+
+        return carry
+
+    lax.fori_loop(0, 6, step, 0)
     g_plane()
-    lax.fori_loop(4, 8, merge, 0)
-    send_b(1)
-    lax.fori_loop(8, 12, merge, 0)
-    send_b(3)
+
+    def step_b(i, carry):
+        lax.fori_loop(8 + i * 2, 10 + i * 2, merge, 0)
+        send_b(order(i))
+        return carry
+
+    lax.fori_loop(0, 3, step_b, 0)
     g_z()
-    lax.fori_loop(12, 16, merge, 0)
+    lax.fori_loop(14, 16, merge, 0)
     for half, total in enumerate(collect(z)):
         sum_a[half] = total
 
@@ -478,6 +501,25 @@
     base[:HALO, :] = base[:HALO, :] + low
     high = jnp.where(me == 127, 0.0, rim_in[0].astype(F32))
     base[ROWS - HALO :, :] = base[ROWS - HALO :, :] + high
+    for copy in pending[:early]:
+        copy.wait_send()
+
+    def sent_parts(zc, carry):
+        remote(hubc.at[zc], hubc.at[zc], hc_s.at[zc], hc_r.at[zc], partner).wait_send()
+        for k in range(3):
+            for half in range(2):
+                block = recv_a.at[half, k, zc]
+                remote(block, block, ha_s.at[half, k, zc], ha_r.at[half, k, zc], partner).wait_send()
+        return carry
+
+    def sent_plane(n, carry):
+        remote(gsend.at[y, x], gxy.at[n], gxy_s.at[n], gxy_r.at[n], partner).wait_send()
+        return carry
+
+    lax.fori_loop(0, 4, sent_parts, 0)
+    lax.fori_loop(1, 16, sent_plane, 0)
+    for k in range(3):
+        remote(recv_b.at[k], recv_b.at[k], hb_s.at[k], hb_r.at[k], partner).wait_send()
     total = jnp.concatenate([hub_total(0), hub_total(1)], axis=1)
     upper = total.astype(BF)
     lower = (total - upper.astype(F32)).astype(BF)
@@ -494,8 +536,14 @@
     lax.fori_loop(0, 8, finish, 0)
     g_done()
     sums[...] = gall[...]
-    for copy in pending:
+    for copy in pending[early:]:
         copy.wait_send()
+
+    def sent_gather(n, carry):
+        remote(gall.at[c, y, x], gall.at[c, y, x], gg_s.at[n], gg_r.at[n], partner).wait_send()
+        return carry
+
+    lax.fori_loop(1, 16, sent_gather, 0)
 
 
 def deliver(hid, fgrad, gall, hidden_out, grad_out, self_out, neighbor_out, bias_out, sem):
@@ -503,10 +551,11 @@
     for copy in copies:
         copy.start()
     for which, out in ((0, self_out), (1, neighbor_out)):
-        out[:, :TILE] = gall[which, :, :, 0:16, :].reshape(WIDTH, TILE)
-        out[:, TILE:] = gall[which, :, :, 16:32, :].reshape(WIDTH, TILE)
-    bias_out[:, :TILE] = gall[0, 0, 0, 32:33, :]
-    bias_out[:, TILE:] = gall[0, 0, 0, 33:34, :]
+        out[:, :TILE] = gall[which, :, :, 0:16, :].astype(F32).reshape(WIDTH, TILE)
+        out[:, TILE:] = gall[which, :, :, 16:32, :].astype(F32).reshape(WIDTH, TILE)
+    bias_row = gall[0, 0, 0, 32:40, :].astype(F32)
+    bias_out[:, :TILE] = bias_row[0:1, :]
+    bias_out[:, TILE:] = bias_row[1:2, :]
     for copy in copies:
         copy.wait()
 
@@ -550,9 +599,10 @@
     VMEM((2, 4, 4, 40, TILE), F32),
     VMEM((4, 4, 40, TILE), F32),
     VMEM((4, 4, 40, TILE), F32),
-    VMEM((15, 40, TILE), F32),
+    VMEM((4, 4, 48, TILE), BF),
+    VMEM((16, 48, TILE), BF),
     VMEM((4, 40, TILE), F32),
-    VMEM((2, 4, 4, 40, TILE), F32),
+    VMEM((2, 4, 4, 48, TILE), BF),
     DMA((8,)), DMA((TILES,)),
     DMA((2,)), DMA((2,)),
     DMA((2, 2, 3)), DMA((2, 2, 3)),
@@ -562,9 +612,9 @@
     DMA((4,)), DMA((4,)),
     DMA((2, 3, 4)), DMA((2, 3, 4)), DMA((3,)), DMA((3,)), DMA((2, 3)), DMA((2, 3)),
     DMA((1,)), DMA((1,)),
-    DMA((15,)), DMA((15,)),
+    DMA((16,)), DMA((16,)),
     DMA((3,)), DMA((3,)),
-    DMA((15,)), DMA((15,)),
+    DMA((16,)), DMA((16,)),
     DMA((1,)), DMA((1,)),
 ]
 
@@ -579,7 +629,7 @@
     wide = jax.ShapeDtypeStruct((ROWS, WIDTH), BF)
     hidden, feature_grad, sums = pl.pallas_call(
         kernel,
-        out_shape=(VMEM(wide.shape, BF), VMEM(wide.shape, BF), VMEM((2, 4, 4, 40, TILE), F32)),
+        out_shape=(VMEM(wide.shape, BF), VMEM(wide.shape, BF), VMEM((2, 4, 4, 48, TILE), BF)),
         in_specs=[smem, smem] + [hbm] * 9,
         out_specs=(vmem, vmem, vmem),
         scratch_shapes=SCRATCH,

time: 68.7 us -> 63.1 us (0.918)
  Pallas kernels: 67.1 us -> 62 us
    pallas_call x1, Pallas kernels: 64.9 us -> 59.8 us  [local(): pl.pallas_call(kernel, out_shape=(VMEM(wide.shape, BF), VMEM(wide.shape,...]
where the time goes in v3:
time: 63.1 us; the launch traced here: 62.6 us
  Pallas kernels  62 us (98%)
  between operations  0.64 us (1%)
    pallas_call x1, Pallas kernels, local(): pl.pallas_call(kernel, out_shape=(VMEM(wide.shape, BF), VMEM(wide.shape,...  59.8 us
    pallas_call x1, Pallas kernels, local(): pl.pallas_call(deliver, out_shape=(wide, wide, square, square, jax.ShapeD...  2.12 us

profile of v3, /device:TPU:1, one launch (start us, length us, event | category | flops | bytes accessed | tf_op | source)
XLA Modules:
  0.0 62.6 jit_solution(10655361661314494456)
XLA Ops:
  0.6 59.8 %sage_layer.1 = (bf16[2048,256]{1,0:T(8,128)(2,1)S(1)}, bf16[2048,256]{1,0:T(8,128)(2,1)S(1)}, bf16[2,4,4,48,128]{4,3,2,1,0:T(8,128)(2,1)S(1)}) custom-call(s32[6,16]{1,0:T(8,128)} %bitcast.11, s32[32]{0:T(128)} %hrow.1, bf16[16,128,256]{2,1,0:T(8,128)(2,1)} %bitcast.7, s32[16,6,128,128]{3,2,1,0:T(8,128)} %bits_hbm.1, bf16[2048,256]{1,0:T(8,128)(2,1)} %cot_hbm.1, ...), custom_call_target="tpu_custom_call" | custom-call | tf_op jit(solution)/shard_map/sage_layer/pallas_call | solution.py:630
  60.5 2.1 %deliver.1 = (bf16[2048,256]{1,0:T(8,128)(2,1)}, bf16[2048,256]{1,0:T(8,128)(2,1)}, f32[256,256]{1,0:T(8,128)}, f32[256,256]{1,0:T(8,128)}, f32[1,256]{1,0:T(1,128)}) custom-call(bf16[2048,256]{1,0:T(8,128)(2,1)S(1)} %get-tuple-element.13.hid, bf16[2048,256]{1,0:T(8,128)(2,1)S(1)} %get-tuple-element.14.fgrad, ...), custom_call_target="tpu_custom_call" | custom-call | tf_op jit(solution)/shard_map/deliver/pallas_call | solution.py:645

commit v4 on v3

--- a/solution.py
+++ b/solution.py
@@ -48,7 +48,7 @@
     rdeg, agg, dpre, dsc, base, rim_out, rim_in,
     hubp, hubc, hubs, recv_a, sum_a, out_b, recv_b, sum_b, recv_c,
     gpart, gcore, gsum, gsend, gxy, gz, gall,
-    load_sem, bits_sem, halo_s, halo_r, ag_s, ag_r, line_s, line_r, core_s, core_r, rim_s, rim_r,
+    load_sem, feat_sem, bits_sem, halo_s, halo_r, ag_s, ag_r, line_s, line_r, core_s, core_r, rim_s, rim_r,
     hc_s, hc_r, ha_s, ha_r, hb_s, hb_r, hd_s, hd_r,
     gc_s, gc_r, gxy_s, gxy_r, gz_s, gz_r, gg_s, gg_r, gh_s, gh_r,
 ):
@@ -63,8 +63,11 @@
         place[dim] = (place[dim] + k) % 4
         return tuple(place)
 
-    load_f = pltpu.make_async_copy(feat_hbm, feat, load_sem.at[0])
-    load_f.start()
+    load_f = [
+        pltpu.make_async_copy(feat_hbm.at[q * 4 : q * 4 + 4], feat.at[q * 4 : q * 4 + 4], feat_sem.at[q]) for q in range(4)
+    ]
+    for load in load_f:
+        load.start()
     small = [
         pltpu.make_async_copy(source, target, load_sem.at[2 + i])
         for i, (source, target) in enumerate(
@@ -83,9 +86,7 @@
     bit_loads = []
     for r in range(TILES):
         load = pltpu.make_async_copy(bits_hbm.at[r], bits.at[r], bits_sem.at[r])
-        load.start()
         bit_loads.append(load)
-    load_c.start()
 
     lane = lax.broadcasted_iota(I32, (32, TILE), 1)
     sub = lax.broadcasted_iota(I32, (32, TILE), 0)
@@ -99,8 +100,12 @@
     pick = jnp.concatenate(
         [(hub_col == lane + j * TILE).astype(F32).astype(BF) for j in range(TILES)], axis=1
     )
-    load_f.wait()
-    own = jnp.dot(pick, feat[...].reshape(ROWS, WIDTH), preferred_element_type=F32).astype(BF)
+    own = jnp.zeros((32, WIDTH), F32)
+    for q in range(4):
+        load_f[q].wait()
+        rows = feat[q * 4 : q * 4 + 4].reshape(512, WIDTH)
+        own = own + jnp.dot(pick[:, q * 512 : q * 512 + 512], rows, preferred_element_type=F32)
+    own = own.astype(BF)
     table[0, z, x, y, c] = own[:, :TILE]
     table[1, z, x, y, c] = own[:, TILE:]
 
@@ -154,6 +159,9 @@
 
     gather_send(0, 0)
     gather_send(0, 1)
+    for load in bit_loads:
+        load.start()
+    load_c.start()
 
     for load in small:
         load.wait()
@@ -176,7 +184,7 @@
                 keep = jnp.broadcast_to(jnp.where(slot_high[k : k + 1, cols] == h, 1.0, 0.0), (16, span)).astype(BF)
                 keep = jnp.broadcast_to(keep[None], (16, 16, span)).reshape(256, span)
                 total = total + onehot[k] * keep
-            counts[rows_at(h * 256, 256), cols] = total
+            counts[h // 4, pl.ds((h % 4) * 4, 4), :, :, cols] = total.reshape(4, 2, 32, span)
             return carry
 
         return lax.fori_loop(0, HUBS // 256, block, carry)
@@ -232,6 +240,19 @@
     for half in range(2):
         core_send(line_recv(half, 2), n)
         n += 1
+
+    def hub_terms(core, add):
+        def nodes(j, carry):
+            cols = rows_at(j * 1024, 1024)
+            right = jnp.concatenate([table[half, :, :, :, core].reshape(HUBS // 2, TILE) for half in range(2)], axis=1)
+            left = counts[:, :, core, :, cols].reshape(HUBS // 2, 1024)
+            value = lax.dot_general(left, right, TN, preferred_element_type=F32)
+            base[cols, :] = base[cols, :] + value if add else value
+            return carry
+
+        lax.fori_loop(0, 2, nodes, 0)
+
+    hub_terms(c, False)
     low[2:6] = feat[0:4]
     high[0:4] = feat[12:16]
     halo_low.wait_recv()
@@ -251,35 +272,29 @@
 
     load_c.wait()
 
-    def layer(j, carry):
-        cols = rows_at(j * 1024, 1024)
-        right = jnp.concatenate([table[0].reshape(HUBS, TILE), table[1].reshape(HUBS, TILE)], axis=1)
-        base[cols, :] = lax.dot_general(counts[:, cols], right, TN, preferred_element_type=F32)
-
-        def chunk(i, carry):
-            start = j * 1024 + i * 256
-            here = rows_at(start, 256)
-            for s in range(4):
-                part = rows_at(start + s * 64, 64)
-                scale = rdeg[part, :]
-                total = band[part, :] + base[part, :]
-                agg[part, :] = (total * jnp.concatenate([scale, scale], axis=1)).astype(BF)
-            pre = pre0[here, :] + jnp.dot(agg[here, :], wn[...], preferred_element_type=F32)
-            for s in range(4):
-                part = rows_at(start + s * 64, 64)
-                v = pre[s * 64 : s * 64 + 64, :]
-                sig = 1.0 / (1.0 + jnp.exp(-v))
-                act = v * sig
-                hid[part, :] = act.astype(BF)
-                dpre[part, :] = (cot[part, :].astype(F32) * sig * (1.0 + v - act)).astype(BF)
-            back = lax.dot_general(dpre[here, :], wn[...], NT, preferred_element_type=F32)
-            scale = rdeg[here, :]
-            dsc[rows_at(512 + start, 256), :] = (back * jnp.concatenate([scale, scale], axis=1)).astype(BF)
-            return carry
-
-        return lax.fori_loop(0, 4, chunk, carry)
-
-    lax.fori_loop(0, 2, layer, 0)
+    def layer(i, carry):
+        start = i * 512
+        here = rows_at(start, 512)
+        for s in range(8):
+            part = rows_at(start + s * 64, 64)
+            scale = rdeg[part, :]
+            total = band[part, :] + base[part, :]
+            agg[part, :] = (total * jnp.concatenate([scale, scale], axis=1)).astype(BF)
+        pre = pre0[here, :] + jnp.dot(agg[here, :], wn[...], preferred_element_type=F32)
+        for s in range(8):
+            part = rows_at(start + s * 64, 64)
+            v = pre[s * 64 : s * 64 + 64, :]
+            sig = 0.5 * jnp.tanh(0.5 * v) + 0.5
+            act = v * sig
+            hid[part, :] = act.astype(BF)
+            dpre[part, :] = (cot[part, :].astype(F32) * sig * (1.0 + v - act)).astype(BF)
+        back = lax.dot_general(dpre[here, :], wn[...], NT, preferred_element_type=F32)
+        scale = rdeg[here, :]
+        dsc[rows_at(512 + start, 512), :] = (back * jnp.concatenate([scale, scale], axis=1)).astype(BF)
+        return carry
+
+    hub_terms(1 - c, True)
+    lax.fori_loop(0, 4, layer, 0)
 
     gpart[:, :, :, 32:40, :] = jnp.zeros((2, 4, 4, 8, TILE), F32)
     for which, left in ((0, feat[...].reshape(ROWS, WIDTH)), (1, agg[...])):
@@ -352,7 +367,7 @@
         remote(slot, slot, gh_s.at[0], gh_r.at[0], partner).wait_recv()
 
     def hub_part(zc):
-        left = counts[rows_at(zc * 1024, 1024), :]
+        left = counts[zc].reshape(1024, ROWS)
         value = jnp.dot(left, dsc[512 : 512 + ROWS, :], preferred_element_type=F32)
         hubp[zc] = value.astype(BF).reshape(4, 4, 2, 32, WIDTH)
         remote(hubp.at[zc, :, :, 1 - c], hubc.at[zc], hc_s.at[zc], hc_r.at[zc], partner).start()
@@ -547,7 +562,11 @@
 
 
 def deliver(hid, fgrad, gall, hidden_out, grad_out, self_out, neighbor_out, bias_out, sem):
-    copies = [pltpu.make_async_copy(hid, hidden_out, sem.at[0]), pltpu.make_async_copy(fgrad, grad_out, sem.at[1])]
+    copies = []
+    for i, (source, target) in enumerate(((hid, hidden_out), (fgrad, grad_out))):
+        for q in range(4):
+            rows = pl.ds(q * 512, 512)
+            copies.append(pltpu.make_async_copy(source.at[rows], target.at[rows], sem.at[i * 4 + q]))
     for copy in copies:
         copy.start()
     for which, out in ((0, self_out), (1, neighbor_out)):
@@ -573,7 +592,7 @@
     VMEM((4, ROWS), I32),
     VMEM((TILES, TILE), I32),
     VMEM((2, 4, 4, 4, 2, 32, TILE), BF),
-    VMEM((HUBS, ROWS), BF),
+    VMEM((4, 16, 2, 32, ROWS), BF),
     VMEM((4, ROWS), I32),
     VMEM((4, ROWS), I32),
     VMEM((4, 256, 512), BF),
@@ -603,7 +622,7 @@
     VMEM((16, 48, TILE), BF),
     VMEM((4, 40, TILE), F32),
     VMEM((2, 4, 4, 48, TILE), BF),
-    DMA((8,)), DMA((TILES,)),
+    DMA((8,)), DMA((4,)), DMA((TILES,)),
     DMA((2,)), DMA((2,)),
     DMA((2, 2, 3)), DMA((2, 2, 3)),
     DMA((2, 4, 3)), DMA((2, 4, 3)),
@@ -647,7 +666,7 @@
         out_shape=(wide, wide, square, square, jax.ShapeDtypeStruct((1, WIDTH), F32)),
         in_specs=[vmem, vmem, vmem],
         out_specs=(hbm, hbm, vmem, vmem, vmem),
-        scratch_shapes=[DMA((2,))],
+        scratch_shapes=[DMA((8,))],
         compiler_params=pltpu.CompilerParams(vmem_limit_bytes=8 * 2**20),
         name="deliver",
     )(*(pltpu.with_memory_space_constraint(value, VMEM) for value in (hidden, feature_grad, sums)))

time: 63.1 us -> 60.4 us (0.957)
  Pallas kernels: 62 us -> 59.6 us
    pallas_call x1, Pallas kernels: 59.8 us -> 57.4 us  [local(): pl.pallas_call(kernel, out_shape=(VMEM(wide.shape, BF), VMEM(wide.shape,...]
where the time goes in v4:
time: 60.4 us; the launch traced here: 60.2 us
  Pallas kernels  59.6 us (99%)
  between operations  0.64 us (1%)
    pallas_call x1, Pallas kernels, local(): pl.pallas_call(kernel, out_shape=(VMEM(wide.shape, BF), VMEM(wide.shape,...  57.4 us
    pallas_call x1, Pallas kernels, local(): pl.pallas_call(deliver, out_shape=(wide, wide, square, square, jax.ShapeD...  2.17 us

profile of v4, /device:TPU:1, one launch (start us, length us, event | category | flops | bytes accessed | tf_op | source)
XLA Modules:
  0.0 60.2 jit_solution(16370647977324542002)
XLA Ops:
  0.6 57.4 %sage_layer.1 = (bf16[2048,256]{1,0:T(8,128)(2,1)S(1)}, bf16[2048,256]{1,0:T(8,128)(2,1)S(1)}, bf16[2,4,4,48,128]{4,3,2,1,0:T(8,128)(2,1)S(1)}) custom-call(s32[6,16]{1,0:T(8,128)} %bitcast.11, s32[32]{0:T(128)} %hrow.1, bf16[16,128,256]{2,1,0:T(8,128)(2,1)} %bitcast.7, s32[16,6,128,128]{3,2,1,0:T(8,128)} %bits_hbm.1, bf16[2048,256]{1,0:T(8,128)(2,1)} %cot_hbm.1, ...), custom_call_target="tpu_custom_call" | custom-call | tf_op jit(solution)/shard_map/sage_layer/pallas_call | solution.py:649
  58.1 2.2 %deliver.1 = (bf16[2048,256]{1,0:T(8,128)(2,1)}, bf16[2048,256]{1,0:T(8,128)(2,1)}, f32[256,256]{1,0:T(8,128)}, f32[256,256]{1,0:T(8,128)}, f32[1,256]{1,0:T(1,128)}) custom-call(bf16[2048,256]{1,0:T(8,128)(2,1)S(1)} %get-tuple-element.13.hid, bf16[2048,256]{1,0:T(8,128)(2,1)S(1)} %get-tuple-element.14.fgrad, ...), custom_call_target="tpu_custom_call" | custom-call | tf_op jit(solution)/shard_map/deliver/pallas_call | solution.py:664

commit v5 on v4

--- a/solution.py
+++ b/solution.py
@@ -561,7 +561,7 @@
     lax.fori_loop(1, 16, sent_gather, 0)
 
 
-def deliver(hid, fgrad, gall, hidden_out, grad_out, self_out, neighbor_out, bias_out, sem):
+def deliver(hid, fgrad, gall, hidden_out, grad_out, self_out, neighbor_out, bias_out, square, row, sem):
     copies = []
     for i, (source, target) in enumerate(((hid, hidden_out), (fgrad, grad_out))):
         for q in range(4):
@@ -570,11 +570,17 @@
     for copy in copies:
         copy.start()
     for which, out in ((0, self_out), (1, neighbor_out)):
-        out[:, :TILE] = gall[which, :, :, 0:16, :].astype(F32).reshape(WIDTH, TILE)
-        out[:, TILE:] = gall[which, :, :, 16:32, :].astype(F32).reshape(WIDTH, TILE)
+        square[which, :, :TILE] = gall[which, :, :, 0:16, :].astype(F32).reshape(WIDTH, TILE)
+        square[which, :, TILE:] = gall[which, :, :, 16:32, :].astype(F32).reshape(WIDTH, TILE)
+        copy = pltpu.make_async_copy(square.at[which], out, sem.at[8 + which])
+        copy.start()
+        copies.append(copy)
     bias_row = gall[0, 0, 0, 32:40, :].astype(F32)
-    bias_out[:, :TILE] = bias_row[0:1, :]
-    bias_out[:, TILE:] = bias_row[1:2, :]
+    row[:, :TILE] = bias_row[0:1, :]
+    row[:, TILE:] = bias_row[1:2, :]
+    copy = pltpu.make_async_copy(row, bias_out, sem.at[10])
+    copy.start()
+    copies.append(copy)
     for copy in copies:
         copy.wait()
 
@@ -665,8 +671,8 @@
         deliver,
         out_shape=(wide, wide, square, square, jax.ShapeDtypeStruct((1, WIDTH), F32)),
         in_specs=[vmem, vmem, vmem],
-        out_specs=(hbm, hbm, vmem, vmem, vmem),
-        scratch_shapes=[DMA((8,))],
+        out_specs=(hbm,) * 5,
+        scratch_shapes=[VMEM((2, WIDTH, WIDTH), F32), VMEM((1, WIDTH), F32), DMA((11,))],
         compiler_params=pltpu.CompilerParams(vmem_limit_bytes=8 * 2**20),
         name="deliver",
     )(*(pltpu.with_memory_space_constraint(value, VMEM) for value in (hidden, feature_grad, sums)))

time: 60.4 us -> 59.8 us (0.990)
  no operation moved by 1% of the time
where the time goes in v5:
time: 59.8 us; the launch traced here: 59.6 us
  Pallas kernels  59 us (99%)
  between operations  0.64 us (1%)
    pallas_call x1, Pallas kernels, local(): pl.pallas_call(kernel, out_shape=(VMEM(wide.shape, BF), VMEM(wide.shape,...  57.4 us
    pallas_call x1, Pallas kernels, local(): pl.pallas_call(deliver, out_shape=(wide, wide, square, square, jax.ShapeD...  1.58 us

profile of v5, /device:TPU:1, one launch (start us, length us, event | category | flops | bytes accessed | tf_op | source)
XLA Modules:
  0.0 59.6 jit_solution(11168093351033637175)
XLA Ops:
  0.6 57.4 %sage_layer.1 = (bf16[2048,256]{1,0:T(8,128)(2,1)S(1)}, bf16[2048,256]{1,0:T(8,128)(2,1)S(1)}, bf16[2,4,4,48,128]{4,3,2,1,0:T(8,128)(2,1)S(1)}) custom-call(s32[6,16]{1,0:T(8,128)} %bitcast.11, s32[32]{0:T(128)} %hrow.1, bf16[16,128,256]{2,1,0:T(8,128)(2,1)} %bitcast.7, s32[16,6,128,128]{3,2,1,0:T(8,128)} %bits_hbm.1, bf16[2048,256]{1,0:T(8,128)(2,1)} %cot_hbm.1, ...), custom_call_target="tpu_custom_call" | custom-call | tf_op jit(solution)/shard_map/sage_layer/pallas_call | solution.py:655
  58.1 1.6 %deliver.1 = (bf16[2048,256]{1,0:T(8,128)(2,1)}, bf16[2048,256]{1,0:T(8,128)(2,1)}, f32[256,256]{1,0:T(8,128)}, f32[256,256]{1,0:T(8,128)}, f32[1,256]{1,0:T(1,128)}) custom-call(bf16[2048,256]{1,0:T(8,128)(2,1)S(1)} %get-tuple-element.13.hid, bf16[2048,256]{1,0:T(8,128)(2,1)S(1)} %get-tuple-element.14.fgrad, ...), custom_call_target="tpu_custom_call" | custom-call | tf_op jit(solution)/shard_map/deliver/pallas_call | solution.py:670
